TPU v7x, 32 devices: a whole 2x2x4 slice. The times are simulated.
32 devices in a mesh: fsdp: 4 (over x, core), seq: 8 (over z, y).
Axes of the slice: x: 2, y: 2, z: 4, core: 2. Of those that a mesh axis runs over, the one named last changes fastest.
Arguments:
- tiles: bfloat16 [4, 4096, 768], P('fsdp', 'seq'), may hold values from -6 to 6
- documents: int32 [4, 4096], P('fsdp', 'seq'), may hold values from 0 to 3, never falling along the last dimension, each value on 1 to 2048 neighbouring positions
- cotangent: bfloat16 [4, 4096, 768], P('fsdp', 'seq'), may hold values from -6 to 6
- w_qkv: bfloat16 [768, 2304], P('fsdp'), may hold values from -0.21875 to 0.21875
- w_out: bfloat16 [768, 768], P('fsdp'), may hold values from -4 to 4
- w_up: bfloat16 [768, 3072], P('fsdp'), may hold values from -0.21875 to 0.21875
- w_down: bfloat16 [3072, 768], P('fsdp'), may hold values from -0.109375 to 0.109375
- gains: bfloat16 [2, 768], P(None, 'fsdp'), may hold values from 0.5 to 1.5
- shifts: bfloat16 [6, 768], P(None, 'fsdp'), may hold values from -1.5 to 1.5
- hidden_bias: bfloat16 [3072], P('fsdp'), may hold values from -3 to 3
Outputs:
- encoded: bfloat16 [4, 4096, 768], P('fsdp', 'seq')
- grad_tiles: bfloat16 [4, 4096, 768], P('fsdp', 'seq')
- grad_qkv: float32 [768, 2304], P('fsdp')
- grad_out_proj: float32 [768, 768], P('fsdp')
- grad_up: float32 [768, 3072], P('fsdp')
- grad_down: float32 [3072, 768], P('fsdp')
- grad_gains: float32 [2, 768], P(None, 'fsdp')
- grad_shifts: float32 [6, 768], P(None, 'fsdp')
- grad_hidden_bias: float32 [3072], P('fsdp')
Inputs may be any that keep to these rules, and one draw needn't show every extreme that they name: `documents`: 4 slides packed in each sequence: ids never fall along a sequence, each slide has at least one token and at most half of the sequence's tokens, and one slide of each sequence has exactly half of them.
All inputs are finite; a program needn't handle non-finite values.
Results may differ from a plain program's by a relative error of at most 0.014.
Values may be sent and summed in bfloat16 or wider, within the bound.
No kernel may reach another device: no remote copies, remote signals or barrier semaphores. Data moves between devices by JAX's collectives and lax.ppermute only.
A program may use at most 320 MiB of HBM per device.

v0:
```python
import math

import jax
import jax.numpy as jnp
from jax import lax
from jax.sharding import PartitionSpec as P

HEADS = 16
SEG_BASE = 1024
BRANCHES = 5


epsilon = 1e-05
masked = -1e30
shard_dims = (0, 0, 0, 0, 1, 1, 0)


def shortened(array):
    return jax.tree.map(lambda a: a.astype(jnp.bfloat16) if a.dtype == jnp.float32 else a, array)


def swapped(array, axis, bit):
    return lax.ppermute(array, axis, [(i, i ^ 1 << bit) for i in range(lax.axis_size(axis))])


def layer_norm(values, gain_row, shift_row):
    center = jnp.mean(values, axis=-1, keepdims=True)
    centered = values - center
    variance = jnp.mean(centered * centered, axis=-1, keepdims=True)
    return centered * lax.rsqrt(variance + epsilon) * gain_row + shift_row


def gelu_exact(values):
    return jax.nn.gelu(values, approximate=False)


def picker(dilation, head_count):
    return jnp.arange(dilation)[:, None] == (jnp.arange(head_count) % dilation)[None, :]


def select_rows(tensor, dilation, chosen):
    shaped = tensor.reshape((tensor.shape[0] // dilation, dilation) + tensor.shape[1:])
    factors = chosen.reshape(chosen.shape + (1,) * (tensor.ndim - 2)).astype(tensor.dtype)
    return jnp.sum(shaped * factors, axis=1)


def select_docs(doc_ids, dilation, chosen):
    shaped = doc_ids.reshape(doc_ids.shape[0] // dilation, dilation, 1)
    return jnp.sum(shaped * chosen.astype(jnp.int32)[None], axis=1)


def spread_rows(tensor, dilation, chosen):
    factors = chosen.reshape(chosen.shape + (1,) * (tensor.ndim - 2)).astype(tensor.dtype)
    grown_rows = tensor[:, None] * factors
    return grown_rows.reshape((tensor.shape[0] * dilation,) + tensor.shape[1:])


def head_blocks(tensor, per_block):
    moved_axes = jnp.moveaxis(tensor, 1, 0)
    return moved_axes.reshape((moved_axes.shape[0] // per_block, per_block) + moved_axes.shape[1:])


def head_unblock(tensor):
    joined = tensor.reshape((tensor.shape[0] * tensor.shape[1],) + tensor.shape[2:])
    return jnp.moveaxis(joined, 0, 1)


def group_gather(members, doublings):
    seq_rank = lax.axis_index("seq")
    for bit_index in range(doublings):
        partner = jax.tree.map(
            lambda part, own: part.astype(own.dtype),
            swapped(shortened(members), "seq", bit_index),
            members,
        )
        upper_half = seq_rank // 2**bit_index % 2
        members = tuple(
            (
                jnp.where(
                    upper_half == 1,
                    jnp.concatenate([theirs, mine], 0),
                    jnp.concatenate([mine, theirs], 0),
                )
                for mine, theirs in zip(members, partner)
            )
        )
    return members


def group_reduce(members, doublings):
    seq_rank = lax.axis_index("seq")
    for bit_index in reversed(range(doublings)):
        half_rows = members[0].shape[0] // 2
        upper_half = seq_rank // 2**bit_index % 2
        kept_part = tuple(
            (
                jnp.where(upper_half == 1, member[half_rows:], member[:half_rows])
                for member in members
            )
        )
        sent_part = tuple(
            (
                jnp.where(upper_half == 1, member[:half_rows], member[half_rows:])
                for member in members
            )
        )
        received = jax.tree.map(
            lambda part, own: part.astype(own.dtype),
            swapped(shortened(sent_part), "seq", bit_index),
            sent_part,
        )
        members = tuple((mine + theirs for mine, theirs in zip(kept_part, received)))
    return members


def forward_block(pieces):
    queries, key_block, value_block, query_docs, key_docs = pieces
    scaling = queries.shape[-1] ** (-0.5)
    scores = (
        jnp.einsum("hqd,hkd->hqk", queries, key_block, preferred_element_type=jnp.float32) * scaling
    )
    scores = jnp.where(query_docs[:, :, None] == key_docs[:, None, :], scores, masked)
    summit = jnp.max(scores, axis=-1, keepdims=True)
    log_total = summit[..., 0] + jnp.log(jnp.sum(jnp.exp(scores - summit), axis=-1))
    weights = jnp.exp(scores - log_total[..., None])
    output = jnp.einsum(
        "hqk,hkd->hqd",
        weights.astype(jnp.bfloat16),
        value_block,
        preferred_element_type=jnp.float32,
    )
    return (log_total, output)


def backward_block(pieces):
    queries, key_block, value_block, query_docs, key_docs, log_total, grad_log, grad_output = pieces
    scaling = queries.shape[-1] ** (-0.5)
    scores = (
        jnp.einsum("hqd,hkd->hqk", queries, key_block, preferred_element_type=jnp.float32) * scaling
    )
    scores = jnp.where(query_docs[:, :, None] == key_docs[:, None, :], scores, masked)
    weights = jnp.exp(scores - log_total[..., None])
    grad_weights = jnp.einsum(
        "hqd,hkd->hqk", grad_output, value_block, preferred_element_type=jnp.float32
    )
    inner_sum = jnp.sum(weights * grad_weights, axis=-1, keepdims=True)
    grad_scores = (weights * (grad_weights - inner_sum + grad_log[..., None])).astype(jnp.bfloat16)
    grad_queries = (
        jnp.einsum("hqk,hkd->hqd", grad_scores, key_block, preferred_element_type=jnp.float32)
        * scaling
    )
    grad_key_block = (
        jnp.einsum("hqk,hqd->hkd", grad_scores, queries, preferred_element_type=jnp.float32)
        * scaling
    )
    grad_value_block = jnp.einsum(
        "hqk,hqd->hkd",
        weights.astype(jnp.bfloat16),
        grad_output,
        preferred_element_type=jnp.float32,
    )
    return (grad_queries, grad_key_block, grad_value_block)


def pack_flat(gradients, parts):
    columns = []
    for gradient, axis_index in zip(gradients, shard_dims):
        if axis_index == 0:
            columns.append(gradient.reshape(parts, -1))
        else:
            regrouped = gradient.reshape(gradient.shape[0], parts, -1)
            columns.append(jnp.moveaxis(regrouped, 1, 0).reshape(parts, -1))
    return jnp.concatenate(columns, axis=1).reshape(-1)


def unpack(flat_values, shapes):
    pieces = []
    offset = 0
    for shape_entry in shapes:
        entry_len = math.prod(shape_entry)
        pieces.append(flat_values[offset : offset + entry_len].reshape(shape_entry))
        offset = offset + entry_len
    return pieces


def local(tiles, documents, cotangent, w_qkv, w_out, w_up, w_down, gains, shifts, hidden_bias):
    local_params = (w_qkv, w_out, w_up, w_down, gains, shifts, hidden_bias)
    gathered = (
        lax.all_gather(w_qkv, "fsdp", axis=0, tiled=True),
        lax.all_gather(w_out, "fsdp", axis=0, tiled=True),
        lax.all_gather(w_up, "fsdp", axis=0, tiled=True),
        lax.all_gather(w_down, "fsdp", axis=0, tiled=True),
        lax.all_gather(gains, "fsdp", axis=1, tiled=True),
        lax.all_gather(shifts, "fsdp", axis=1, tiled=True),
        lax.all_gather(hidden_bias, "fsdp", axis=0, tiled=True),
    )
    full_qkv, full_out, full_up, full_down, full_gains, full_shifts, full_bias = gathered
    gain_rows = full_gains.astype(jnp.float32)
    shift_rows = full_shifts.astype(jnp.float32)
    bias_row = full_bias.astype(jnp.float32)
    inputs = tiles[0].astype(jnp.float32)
    tok_count, model_width = inputs.shape
    head_count = HEADS
    head_dim = model_width // head_count
    seq_rank = lax.axis_index("seq")
    own_docs = documents[0]
    all_docs = lax.all_gather(own_docs, "seq", axis=0, tiled=True)
    total_len = all_docs.shape[0]
    normed = layer_norm(inputs, gain_rows[0], shift_rows[0])
    normed_low = normed.astype(jnp.bfloat16)
    project = jnp.dot(normed_low, full_qkv, preferred_element_type=jnp.float32)
    shaped = (tok_count, head_count, head_dim)
    queries = (project[:, :model_width] + shift_rows[1]).astype(jnp.bfloat16).reshape(shaped)
    key_all = project[:, model_width : 2 * model_width].astype(jnp.bfloat16).reshape(shaped)
    value_all = (project[:, 2 * model_width :] + shift_rows[2]).astype(jnp.bfloat16).reshape(shaped)
    kept_state = []
    out_list = []
    log_list = []
    for branch in range(BRANCHES):
        dilation = 2**branch
        segment = min(SEG_BASE * dilation, total_len)
        group_size = segment // tok_count
        doublings = group_size.bit_length() - 1
        per_block = min(dilation, head_count)
        chosen = picker(dilation, head_count)
        query_rows = select_rows(queries, dilation, chosen)
        key_rows, value_rows = group_gather(
            (select_rows(key_all, dilation, chosen), select_rows(value_all, dilation, chosen)),
            doublings,
        )
        key_count = segment // dilation
        first_row = seq_rank // group_size * key_count
        doc_table = all_docs.reshape(total_len // dilation, dilation)
        key_docs = select_docs(
            lax.dynamic_slice_in_dim(doc_table, first_row, key_count, 0).reshape(-1),
            dilation,
            chosen,
        )
        query_docs = select_docs(own_docs, dilation, chosen)
        blocks = (
            head_blocks(query_rows, per_block),
            head_blocks(key_rows, per_block),
            head_blocks(value_rows, per_block),
            head_blocks(query_docs, per_block),
            head_blocks(key_docs, per_block),
        )
        block_logs, block_outs = lax.map(forward_block, blocks)
        branch_logs = head_unblock(block_logs)
        branch_outs = head_unblock(block_outs)
        out_list.append(spread_rows(branch_outs, dilation, chosen))
        log_list.append(
            jnp.where(chosen[None], branch_logs[:, None, :], masked).reshape(tok_count, head_count)
        )
        kept_state.append((blocks, block_logs, dilation, chosen, per_block, doublings))
    log_stack = jnp.stack(log_list)
    summit = jnp.max(log_stack, axis=0)
    log_all = summit + jnp.log(jnp.sum(jnp.exp(log_stack - summit), axis=0))
    shares = [jnp.exp(log_entry - log_all) for log_entry in log_list]
    merged_out = shares[0][..., None] * out_list[0]
    for branch in range(1, BRANCHES):
        merged_out = merged_out + shares[branch][..., None] * out_list[branch]
    merged_low = merged_out.reshape(tok_count, model_width).astype(jnp.bfloat16)
    attended = jnp.dot(merged_low, full_out, preferred_element_type=jnp.float32) + shift_rows[3]
    middle = inputs + attended
    normed_two = layer_norm(middle, gain_rows[1], shift_rows[4])
    normed_two_low = normed_two.astype(jnp.bfloat16)
    hidden = jnp.dot(normed_two_low, full_up, preferred_element_type=jnp.float32) + bias_row
    active_low = gelu_exact(hidden).astype(jnp.bfloat16)
    result = (
        middle + jnp.dot(active_low, full_down, preferred_element_type=jnp.float32) + shift_rows[5]
    )
    back_params = (
        lax.all_gather(w_qkv, "fsdp", axis=0, tiled=True),
        lax.all_gather(w_out, "fsdp", axis=0, tiled=True),
        lax.all_gather(w_up, "fsdp", axis=0, tiled=True),
        lax.all_gather(w_down, "fsdp", axis=0, tiled=True),
        lax.all_gather(gains, "fsdp", axis=1, tiled=True),
        lax.all_gather(shifts, "fsdp", axis=1, tiled=True),
        lax.all_gather(hidden_bias, "fsdp", axis=0, tiled=True),
    )
    back_qkv = back_params[0]
    back_out = back_params[1]
    back_up = back_params[2]
    back_down = back_params[3]
    grad_in = cotangent[0]
    grad_result = grad_in.astype(jnp.float32)
    grad_down = jnp.einsum("tf,td->fd", active_low, grad_in, preferred_element_type=jnp.float32)
    grad_shift_down = jnp.sum(grad_result, axis=0)
    grad_active = jnp.einsum("td,fd->tf", grad_in, back_down, preferred_element_type=jnp.float32)
    gelu_pull = jax.vjp(gelu_exact, hidden)[1]
    grad_hidden_low = gelu_pull(grad_active)[0].astype(jnp.bfloat16)
    grad_up = jnp.einsum(
        "td,tf->df", normed_two_low, grad_hidden_low, preferred_element_type=jnp.float32
    )
    grad_bias = jnp.sum(grad_hidden_low.astype(jnp.float32), axis=0)
    grad_normed_two = jnp.einsum(
        "tf,df->td", grad_hidden_low, back_up, preferred_element_type=jnp.float32
    )
    norm_pull_two = jax.vjp(layer_norm, middle, gain_rows[1], shift_rows[4])[1]
    grad_middle_part, grad_gain_two, grad_shift_two = norm_pull_two(grad_normed_two)
    grad_middle = grad_result + grad_middle_part
    grad_attended_low = grad_middle.astype(jnp.bfloat16)
    grad_out = jnp.einsum(
        "td,te->de", merged_low, grad_attended_low, preferred_element_type=jnp.float32
    )
    grad_shift_out = jnp.sum(grad_attended_low.astype(jnp.float32), axis=0)
    grad_merged = jnp.einsum(
        "te,de->td", grad_attended_low, back_out, preferred_element_type=jnp.float32
    ).reshape(shaped)
    merged_dot = jnp.sum(grad_merged * merged_out, axis=-1)
    grad_query_full = jnp.zeros(shaped, jnp.float32)
    grad_key_full = jnp.zeros(shaped, jnp.float32)
    grad_value_full = jnp.zeros(shaped, jnp.float32)
    for branch in range(BRANCHES):
        blocks, block_logs, dilation, chosen, per_block, doublings = kept_state[branch]
        branch_share = shares[branch]
        alignment = jnp.sum(grad_merged * out_list[branch], axis=-1) - merged_dot
        grad_log_rows = select_rows(branch_share * alignment, dilation, chosen)
        grad_rows_low = select_rows(branch_share[..., None] * grad_merged, dilation, chosen).astype(
            jnp.bfloat16
        )
        back_pieces = blocks + (
            block_logs,
            head_blocks(grad_log_rows, per_block),
            head_blocks(grad_rows_low, per_block),
        )
        grad_q_blocks, grad_k_blocks, grad_v_blocks = lax.map(backward_block, back_pieces)
        grad_key_rows, grad_value_rows = group_reduce(
            (head_unblock(grad_k_blocks), head_unblock(grad_v_blocks)), doublings
        )
        grad_query_full = grad_query_full + spread_rows(
            head_unblock(grad_q_blocks), dilation, chosen
        )
        grad_key_full = grad_key_full + spread_rows(grad_key_rows, dilation, chosen)
        grad_value_full = grad_value_full + spread_rows(grad_value_rows, dilation, chosen)
    flat_shape = (tok_count, model_width)
    grad_project_low = jnp.concatenate(
        [
            grad_query_full.reshape(flat_shape),
            grad_key_full.reshape(flat_shape),
            grad_value_full.reshape(flat_shape),
        ],
        axis=1,
    ).astype(jnp.bfloat16)
    grad_qkv = jnp.einsum(
        "td,te->de", normed_low, grad_project_low, preferred_element_type=jnp.float32
    )
    grad_project = grad_project_low.astype(jnp.float32)
    grad_shift_query = jnp.sum(grad_project[:, :model_width], axis=0)
    grad_shift_value = jnp.sum(grad_project[:, 2 * model_width :], axis=0)
    grad_normed = jnp.einsum(
        "te,de->td", grad_project_low, back_qkv, preferred_element_type=jnp.float32
    )
    norm_pull_one = jax.vjp(layer_norm, inputs, gain_rows[0], shift_rows[0])[1]
    grad_input_part, grad_gain_one, grad_shift_one = norm_pull_one(grad_normed)
    grad_inputs = grad_middle + grad_input_part
    grad_gains = jnp.stack([grad_gain_one, grad_gain_two])
    grad_shifts = jnp.stack(
        [
            grad_shift_one,
            grad_shift_query,
            grad_shift_value,
            grad_shift_out,
            grad_shift_two,
            grad_shift_down,
        ]
    )
    gradients = (grad_qkv, grad_out, grad_up, grad_down, grad_gains, grad_shifts, grad_bias)
    packed = pack_flat(gradients, lax.axis_size("fsdp"))
    narrow = lax.psum_scatter(
        packed.astype(jnp.bfloat16), "fsdp", scatter_dimension=0, tiled=True
    ).astype(jnp.float32)
    piece = lax.psum_scatter(narrow, "seq", scatter_dimension=0, tiled=True)
    reduced = lax.all_gather(piece.astype(jnp.bfloat16), "seq", axis=0, tiled=True).astype(
        piece.dtype
    )
    pieces = unpack(reduced, [member.shape for member in local_params])
    return (
        result.astype(jnp.bfloat16)[None],
        grad_inputs.astype(jnp.bfloat16)[None],
        pieces[0],
        pieces[1],
        pieces[2],
        pieces[3],
        pieces[4],
        pieces[5],
        pieces[6],
    )


def solution(mesh):
    return jax.shard_map(
        local,
        mesh=mesh,
        in_specs=(
            P("fsdp", "seq", None),
            P("fsdp", "seq"),
            P("fsdp", "seq", None),
            P("fsdp", None),
            P("fsdp", None),
            P("fsdp", None),
            P("fsdp", None),
            P(None, "fsdp"),
            P(None, "fsdp"),
            P("fsdp"),
        ),
        out_specs=(
            P("fsdp", "seq", None),
            P("fsdp", "seq", None),
            P("fsdp", None),
            P("fsdp", None),
            P("fsdp", None),
            P("fsdp", None),
            P(None, "fsdp"),
            P(None, "fsdp"),
            P("fsdp"),
        ),
        check_vma=False,
    )
```

profile of v0, /device:TPU:0, one launch (start us, length us, event | category | flops | bytes accessed | tf_op | source)
XLA Modules:
  0.0 2040.1 jit_solution(1918747673582172182)
XLA Ops:
  11.2 27.8 %all-gather = s32[1,4096]{1,0:T(1,128)S(1)} all-gather(s32[1,512]{1,0:T(1,128)S(1)} %copy-done.146), channel_id=2, replica_groups=mesh['fsdp'=4,'seq'=8] {'seq'}, dimensions={1}, use_global_device_ids=true | all-gather | bytes 18432 | tf_op jit(solution)/shard_map/all_gather | solution.py:207
  45.5 5.2 all-gather.2
  51.4 5.1 all-gather.1
  71.8 5.2 all-gather.3
  81.0 4.2 fusion.340
  107.8 7.7 multiply_reduce_fusion.14
  140.6 6.6 multiply_reduce_fusion.11
  153.3 6.9 multiply_reduce_fusion.17
  192.0 5.2 collective-permute-done.19
  197.4 6.6 collective-permute-done.22
  217.0 6.9 collective-permute-done.20
  224.6 7.3 collective-permute-done.23
  258.1 4.6 collective-permute-done.7
  263.8 5.8 collective-permute-done.17
  269.7 9.6 collective-permute-done.14
  310.8 58.6 %while.115 = (s32[]{:T(128)}, f32[16,1,512]{2,1,0:T(1,128)S(1)}, f32[16,1,512,48]{2,3,1,0:T(8,128)S(1)}, s32[16,1,512]{2,1,0:T(1,128)S(1)}, s32[16,1,1024]{2,1,0...) while((s32[]{:T(128)}, f32[16,1,512]{2,1,0:T(1,128)S(1)}, ...), condition=%wide.region_5.6_spmd, body=%wide.region_2.0_spmd.sunk | while | flops 104857088 | bytes 7084137 | solution.py:247
  378.8 31.4 %while.116 = (s32[]{:T(128)}, f32[8,2,256]{2,1,0:T(2,128)S(1)}, f32[8,2,256,48]{2,3,1,0:T(8,128)}, s32[8,2,256]{2,1,0:T(2,128)}, s32[8,2,1024]{2,1,0:T(2,128)S(1...) while((s32[]{:T(128)}, f32[8,2,256]{2,1,0:T(2,128)S(1)}, ...), condition=%wide.region_14.15_spmd, body=%wide.region_11.14_spmd.sunk | while | flops 104857088 | bytes 6881385 | solution.py:247
  420.0 4.7 mul.1262
  438.8 18.8 while.117
  474.4 4.7 mul.1272
  498.7 21.1 %multiply_convert_fusion.3 = (bf16[512,3072]{1,0:T(8,128)(2,1)}, f32[512,3072]{1,0:T(8,128)}, f32[512,3072]{1,0:T(8,128)}) fusion(f32[3072]{0:T(1024)S(1)} %bitcast.1012, bf16[768,3072]{1,0:T(8,128)(2,1)} %all-gather.13.cloned.1.call-done, f32[512,768]{1,0:T(8,128)} %copy-done.38, f32[768]{0:T(1024)S(1)} %copy-done.197, f32[768]{0:T(1024)S(1)} %copy-done.180, ...), kind=kOutput, calls=%fused_computation.256 | convolution fusion | flops 2521694208 | bytes 22042624 | tf_op jit(solution)/shard_map/dot_general | solution.py:267
  519.8 9.2 fusion.360
  551.8 7.6 convolution_convert_fusion.1
  565.7 173.7 %while.119 = (s32[]{:T(128)}, f32[16,1,512,48]{2,3,1,0:T(8,128)S(1)}, f32[16,1,1024,48]{2,3,1,0:T(8,128)}, f32[16,1,1024,48]{2,3,1,0:T(8,128)}, s32[16,1,512]{2,...) while((s32[]{:T(128)}, ...), condition=%wide.region_49.50_spmd, body=%wide.region_47.49_spmd.sunk | while | flops 257498624 | bytes 17407116 | solution.py:327
  752.8 119.4 %while.120 = (s32[]{:T(128)}, f32[8,2,256,48]{2,3,1,0:T(8,128)}, f32[8,2,1024,48]{2,3,1,0:T(8,128)}, f32[8,2,1024,48]{2,3,1,0:T(8,128)}, s32[8,2,256]{2,1,0:T(2,...) while((s32[]{:T(128)}, f32[8,2,256,48]{2,3,1,0:T(8,128)}, ...), condition=%wide.region_55.56_spmd, body=%wide.region_53.55_spmd.sunk | while | flops 259648512 | bytes 24790152 | solution.py:327
  763.6 4.1 fusion.488
  778.6 4.1 fusion.488
  793.5 4.1 fusion.488
  808.4 4.1 fusion.488
  880.7 64.0 %while.121 = (s32[]{:T(128)}, f32[4,4,128,48]{2,3,1,0:T(8,128)S(1)}, f32[4,4,1024,48]{2,3,1,0:T(8,128)}, f32[4,4,1024,48]{2,3,1,0:T(8,128)}, s32[4,4,128]{2,1,0:...) while((s32[]{:T(128)}, f32[4,4,128,48]{2,3,1,0:T(8,128)S(1)}, ...), condition=%wide.region_61.62_spmd, body=%wide.region_59.61_spmd.sunk | while | flops 259746816 | bytes 26190984 | solution.py:327
  887.9 4.2 fusion.505
  903.9 4.3 fusion.505
  919.9 4.2 fusion.505
  936.0 4.2 fusion.505
  955.8 18.0 while.122
  983.4 4.8 fusion.273
  1037.9 8.2 reshape.1941
  1048.0 6.7 convolution_convert_fusion
  1054.7 8.2 reshape.1942
  1064.2 7.1 collective-permute-done.45
  1071.7 5.3 collective-permute-done.34
  1078.4 4.5 collective-permute-done.46
  1083.7 4.8 collective-permute-done.35
  1109.9 9.9 collective-permute-done.42
  1120.1 5.5 collective-permute-done.31
  1125.7 5.5 collective-permute-done.43
  1131.9 5.0 collective-permute-done.32
  1148.5 5.1 mul.1407
  1164.9 7.9 collective-permute-done.37
  1175.2 9.3 collective-permute-done.39
  1201.9 4.7 mul.1387
  1240.1 4.9 mul.1404
  1248.4 11.6 fusion.253
  1262.6 4.2 convolution_convert_fusion.2
  1267.2 4.8 fusion.346
  1273.9 6.9 reshape.1939
  1280.8 5.6 constant_dynamic-update-slice_fusion.18
  1297.2 39.3 %convert_element_type.672 = bf16[7087104]{0:T(1024)(128)(2,1)} reshape(bf16[4,1771776]{1,0:T(4,128)(2,1)} %constant_dynamic-update-slice_fusion.12) | data formatting | bytes 28348416 | tf_op jit(solution)/shard_map/convert_element_type | solution.py:371
  1340.3 242.8 %all-reduce.9.cloned.1.call-done = bf16[7087104]{0:T(1024)(128)(2,1)} async-done(((bf16[7087104]{0:T(1024)(128)(2,1)}), bf16[7087104]{0:T(1024)(128)(2,1)}) %all-reduce.9.cloned.1.call-update) | async-done | bytes 14174224
  1583.0 5.3 dynamic-slice_convert_fusion
  1588.3 278.8 %all-reduce.10 = bf16[1771776]{0:T(1024)(128)(2,1)S(1)} all-reduce(f32[1771776]{0:T(1024)} %dynamic-slice_convert_fusion), channel_id=4, replica_groups=mesh['fsdp'=4,'seq'=8] {'seq'}, use_global_device_ids=true, to_apply=%region_84.85.clone | all-reduce | flops 1771776 | bytes 10630656
  1868.4 7.2 dynamic-update-slice
  1877.5 8.2 fusion.272
  1887.3 128.0 %all-reduce.7.cloned.1.call-done = bf16[1771776]{0:T(1024)(128)(2,1)} async-done(((bf16[1771776]{0:T(1024)(128)(2,1)}), bf16[1771776]{0:T(1024)(128)(2,1)}) %all-reduce.7.cloned.1.call-update) | async-done | bytes 3543568
  (1390 shorter events, 975.4 us)
Async XLA Ops:
  7.2 73.7 %all-gather.9.cloned.1.call-start = ((), (), s32[]{:S(2)}) async-start(), calls=%async_computation | async-start | bytes 4423680 | tf_op jit(solution)/shard_map/all_gather | solution.py:189
  7.9 36.4 %copy-start.9 = (bf16[1,512,768]{2,1,0:T(8,128)(2,1)S(1)}, bf16[1,512,768]{2,1,0:T(8,128)(2,1)}, u32[]{:S(2)}) copy-start(bf16[1,512,768]{2,1,0:T(8,128)(2,1)} %param.26) | copy-start | bytes 2359300
  7.9 486.7 %all-gather.11.cloned.1.call-start = ((), (), s32[]{:S(2)}) async-start(), calls=%async_computation.1 | async-start | bytes 1474560 | tf_op jit(solution)/shard_map/all_gather | solution.py:190
  8.7 489.9 %all-gather.13.cloned.1.call-start = ((), (), s32[]{:S(2)}) async-start(), calls=%async_computation.2 | async-start | bytes 5898240 | tf_op jit(solution)/shard_map/all_gather | solution.py:191
  9.4 36.0 %copy-start.194 = (bf16[6,192]{1,0:T(8,128)(2,1)S(1)}, bf16[6,192]{1,0:T(8,128)(2,1)}, u32[]{:S(2)}) copy-start(bf16[6,192]{1,0:T(8,128)(2,1)} %param.34) | copy-start | bytes 6916
  9.4 41.9 %copy-start.204 = (bf16[2,192]{1,0:T(2,128)(2,1)S(1)}, bf16[2,192]{1,0:T(2,128)(2,1)}, u32[]{:S(2)}) copy-start(bf16[2,192]{1,0:T(2,128)(2,1)} %param.33) | copy-start | bytes 2308
  9.4 510.3 %all-gather.15.cloned.1.call-start = ((), (), s32[]{:S(2)}) async-start(), calls=%async_computation.3 | async-start | bytes 5898240 | tf_op jit(solution)/shard_map/all_gather | solution.py:192
  10.0 1573.0 %all-reduce.9.cloned.1.call-start = ((), (), s32[]{:S(2)}) async-start(), calls=%async_computation.5 | async-start | bytes 28348416
  115.5 90.3 %collective-permute-start.6 = (bf16[128,16,48]{2,1,0:T(8,128)(2,1)}, bf16[128,16,48]{2,1,0:T(8,128)(2,1)}, u32[]{:S(2)}, u32[]{:S(2)}) collective-permute-start(bf16[128,16,48]{2,1,0:T(8,128)(2,1)} %get-tuple-element.987), channel_id=1, source_target_pairs={{0,1},{1,0},{2,3},{3,2},{4,5},{5,4},{6,7},{7,6},{8,9},{9,8},{10,11... | collective-permute-start | bytes 589832 | tf_op jit(solution)/shard_map/ppermute | solution.py:23
  147.2 40.2 %collective-permute-start.15 = (bf16[64,16,48]{2,1,0:T(8,128)(2,1)}, bf16[64,16,48]{2,1,0:T(8,128)(2,1)}, u32[]{:S(2)}, u32[]{:S(2)}) collective-permute-start(bf16[64,16,48]{2,1,0:T(8,128)(2,1)} %get-tuple-element.983), channel_id=1, source_target_pairs={{0,1},{1,0},{2,3},{3,2},{4,5},{5,4},{6,7},{7,6},{8,9},{9,8},{10,11... | collective-permute-start | bytes 294920 | tf_op jit(solution)/shard_map/ppermute | solution.py:23
  147.7 42.7 %collective-permute-start.12 = (bf16[64,16,48]{2,1,0:T(8,128)(2,1)}, bf16[64,16,48]{2,1,0:T(8,128)(2,1)}, u32[]{:S(2)}, u32[]{:S(2)}) collective-permute-start(bf16[64,16,48]{2,1,0:T(8,128)(2,1)} %get-tuple-element.984), channel_id=1, source_target_pairs={{0,1},{1,0},{2,3},{3,2},{4,5},{5,4},{6,7},{7,6},{8,9},{9,8},{10,11... | collective-permute-start | bytes 294920 | tf_op jit(solution)/shard_map/ppermute | solution.py:23
  152.8 28.1 %collective-permute-start.18 = (bf16[32,16,48]{0,2,1:T(8,128)(2,1)}, bf16[32,16,48]{0,2,1:T(8,128)(2,1)}, u32[]{:S(2)}, u32[]{:S(2)}) collective-permute-start(bf16[32,16,48]{0,2,1:T(8,128)(2,1)} %copy.841), channel_id=1, source_target_pairs={{0,1},{1,0},{2,3},{3,2},{4,5},{5,4},{6,7},{7,6},{8,9},{9,8},{10,11... | collective-permute-start | bytes 147464 | tf_op jit(solution)/shard_map/ppermute | solution.py:23
  162.5 41.8 %collective-permute-start.9 = (bf16[128,16,48]{2,1,0:T(8,128)(2,1)}, bf16[128,16,48]{2,1,0:T(8,128)(2,1)}, u32[]{:S(2)}, u32[]{:S(2)}) collective-permute-start(bf16[128,16,48]{2,1,0:T(8,128)(2,1)} %get-tuple-element.986), channel_id=1, source_target_pairs={{0,1},{1,0},{2,3},{3,2},{4,5},{5,4},{6,7},{7,6},{8,9},{9,8},{10,11... | collective-permute-start | bytes 589832 | tf_op jit(solution)/shard_map/ppermute | solution.py:23
  179.7 24.3 %copy-start.69 = (bf16[256,16,48]{0,2,1:T(8,128)(2,1)S(1)}, bf16[256,16,48]{0,2,1:T(8,128)(2,1)}, u32[]{:S(2)}) copy-start(bf16[256,16,48]{0,2,1:T(8,128)(2,1)} %copy.804) | copy-start | bytes 1179652
  180.9 5.7 collective-permute-start.21
  186.6 109.6 %collective-permute-start.1 = (bf16[512,16,48]{0,2,1:T(8,128)(2,1)}, bf16[512,16,48]{0,2,1:T(8,128)(2,1)}, u32[]{:S(2)}, u32[]{:S(2)}) collective-permute-start(bf16[512,16,48]{0,2,1:T(8,128)(2,1)} %bitcast.87), channel_id=1, source_target_pairs={{0,1},{1,0},{2,3},{3,2},{4,5},{5,4},{6,7},{7,6},{8,9},{9,8},{10,11... | collective-permute-start | bytes 2359304 | tf_op jit(solution)/shard_map/ppermute | solution.py:23
  187.4 117.4 %collective-permute-start = (bf16[512,16,48]{0,2,1:T(8,128)(2,1)}, bf16[512,16,48]{0,2,1:T(8,128)(2,1)}, u32[]{:S(2)}, u32[]{:S(2)}) collective-permute-start(bf16[512,16,48]{0,2,1:T(8,128)(2,1)} %bitcast.84), channel_id=1, source_target_pairs={{0,1},{1,0},{2,3},{3,2},{4,5},{5,4},{6,7},{7,6},{8,9},{9,8},{10,11... | collective-permute-start | bytes 2359304 | tf_op jit(solution)/shard_map/ppermute | solution.py:23
  190.4 6.7 collective-permute-start.19
  197.2 6.9 collective-permute-start.22
  197.4 26.5 %copy-start.132 = (bf16[128,16,48]{0,2,1:T(8,128)(2,1)}, bf16[128,16,48]{0,2,1:T(8,128)(2,1)S(1)}, u32[]{:S(2)}) copy-start(bf16[128,16,48]{0,2,1:T(8,128)(2,1)S(1)} %maximum_select_fusion.21) | copy-start | bytes 589828
  204.0 42.2 %collective-permute-start.4 = (bf16[256,16,48]{0,2,1:T(8,128)(2,1)S(1)}, bf16[256,16,48]{0,2,1:T(8,128)(2,1)}, u32[]{:S(2)}, u32[]{:S(2)}) collective-permute-start(bf16[256,16,48]{0,2,1:T(8,128)(2,1)S(1)} %copy-done.69), channel_id=1, source_target_pairs={{0,1},{1,0},{2,3},{3,2},{4,5},{5,4},{6,7},{7,6},{8,9},{9,8},{10,11... | collective-permute-start | bytes 1179656 | tf_op jit(solution)/shard_map/ppermute | solution.py:23
  204.3 27.6 %copy-start.134 = (bf16[128,16,48]{0,2,1:T(8,128)(2,1)}, bf16[128,16,48]{0,2,1:T(8,128)(2,1)S(1)}, u32[]{:S(2)}) copy-start(bf16[128,16,48]{0,2,1:T(8,128)(2,1)S(1)} %maximum_select_fusion.23) | copy-start | bytes 589828
  204.3 7.0 collective-permute-start.16
  205.9 8.4 collective-permute-start.13
  211.3 12.6 collective-permute-start.20
  214.2 36.2 %collective-permute-start.2 = (bf16[256,16,48]{0,2,1:T(8,128)(2,1)S(1)}, bf16[256,16,48]{0,2,1:T(8,128)(2,1)}, u32[]{:S(2)}, u32[]{:S(2)}) collective-permute-start(bf16[256,16,48]{0,2,1:T(8,128)(2,1)S(1)} %copy.801), channel_id=1, source_target_pairs={{0,1},{1,0},{2,3},{3,2},{4,5},{5,4},{6,7},{7,6},{8,9},{9,8},{10,11... | collective-permute-start | bytes 1179656 | tf_op jit(solution)/shard_map/ppermute | solution.py:23
  223.9 8.0 collective-permute-start.23
  231.9 21.4 %collective-permute-start.10 = (bf16[256,16,48]{0,2,1:T(8,128)(2,1)}, bf16[256,16,48]{0,2,1:T(8,128)(2,1)}, u32[]{:S(2)}, u32[]{:S(2)}) collective-permute-start(bf16[256,16,48]{0,2,1:T(8,128)(2,1)} %maximum_select_fusion.13), channel_id=1, source_target_pairs={{0,2},{1,3},{2,0},{3,1},{4,6},{5,7},{6,4},{7,5},{8,10},{9,11},{10,... | collective-permute-start | bytes 1179656 | tf_op jit(solution)/shard_map/ppermute | solution.py:23
  246.3 16.4 collective-permute-start.7
  250.5 19.1 collective-permute-start.17
  253.3 26.0 %collective-permute-start.14 = (bf16[256,16,48]{0,2,1:T(8,128)(2,1)S(1)}, bf16[256,16,48]{0,2,1:T(8,128)(2,1)S(1)}, u32[]{:S(2)}, u32[]{:S(2)}) collective-permute-start(bf16[256,16,48]{0,2,1:T(8,128)(2,1)S(1)} %copy-done.70), channel_id=1, source_target_pairs={{0,4},{1,5},{2,6},{3,7},{4,0},{5,1},{6,2},{7,3},{8,12},{9,13},{10,... | collective-permute-start | bytes 1179656 | tf_op jit(solution)/shard_map/ppermute | solution.py:23
  262.7 109.0 %collective-permute-start.5 = (bf16[512,16,48]{0,2,1:T(8,128)(2,1)}, bf16[512,16,48]{0,2,1:T(8,128)(2,1)}, u32[]{:S(2)}, u32[]{:S(2)}) collective-permute-start(bf16[512,16,48]{0,2,1:T(8,128)(2,1)} %maximum_select_fusion.7), channel_id=1, source_target_pairs={{0,2},{1,3},{2,0},{3,1},{4,6},{5,7},{6,4},{7,5},{8,10},{9,11},{10,... | collective-permute-start | bytes 2359304 | tf_op jit(solution)/shard_map/ppermute | solution.py:23
  269.5 104.7 %collective-permute-start.3 = (bf16[512,16,48]{0,2,1:T(8,128)(2,1)}, bf16[512,16,48]{0,2,1:T(8,128)(2,1)}, u32[]{:S(2)}, u32[]{:S(2)}) collective-permute-start(bf16[512,16,48]{0,2,1:T(8,128)(2,1)} %maximum_select_fusion.6), channel_id=1, source_target_pairs={{0,2},{1,3},{2,0},{3,1},{4,6},{5,7},{6,4},{7,5},{8,10},{9,11},{10,... | collective-permute-start | bytes 2359304 | tf_op jit(solution)/shard_map/ppermute | solution.py:23
  279.3 153.2 %collective-permute-start.11 = (bf16[512,16,48]{0,2,1:T(8,128)(2,1)}, bf16[512,16,48]{0,2,1:T(8,128)(2,1)}, u32[]{:S(2)}, u32[]{:S(2)}) collective-permute-start(bf16[512,16,48]{0,2,1:T(8,128)(2,1)} %maximum_select_fusion.9), channel_id=1, source_target_pairs={{0,4},{1,5},{2,6},{3,7},{4,0},{5,1},{6,2},{7,3},{8,12},{9,13},{10,... | collective-permute-start | bytes 2359304 | tf_op jit(solution)/shard_map/ppermute | solution.py:23
  296.2 138.9 %collective-permute-start.8 = (bf16[512,16,48]{0,2,1:T(8,128)(2,1)}, bf16[512,16,48]{0,2,1:T(8,128)(2,1)}, u32[]{:S(2)}, u32[]{:S(2)}) collective-permute-start(bf16[512,16,48]{0,2,1:T(8,128)(2,1)} %maximum_select_fusion.8), channel_id=1, source_target_pairs={{0,4},{1,5},{2,6},{3,7},{4,0},{5,1},{6,2},{7,3},{8,12},{9,13},{10,... | collective-permute-start | bytes 2359304 | tf_op jit(solution)/shard_map/ppermute | solution.py:23
  378.8 32.6 %copy-start.192 = (pred[2,16]{1,0:T(4,128)(4,1)S(1)}, pred[2,16]{1,0:T(4,128)(4,1)}, u32[]{:S(2)}) copy-start(pred[2,16]{1,0:T(4,128)(4,1)} %get-tuple-element.1208) | copy-start | bytes 100
  460.0 28.5 %copy-start.33 = (f32[128,4,16]{2,1,0:T(4,128)}, f32[128,4,16]{2,1,0:T(4,128)S(1)}, u32[]{:S(2)}) copy-start(f32[128,4,16]{2,1,0:T(4,128)S(1)} %broadcast_select_fusion.3) | copy-start | bytes 98308
  743.1 442.8 %collective-permute-start.24 = (bf16[512,16,48]{0,2,1:T(8,128)(2,1)}, bf16[512,16,48]{0,2,1:T(8,128)(2,1)}, u32[]{:S(2)}, u32[]{:S(2)}) collective-permute-start(bf16[512,16,48]{0,2,1:T(8,128)(2,1)} %select_convert_fusion.5), channel_id=1, source_target_pairs={{0,1},{1,0},{2,3},{3,2},{4,5},{5,4},{6,7},{7,6},{8,9},{9,8},{10,11... | collective-permute-start | bytes 2359304 | tf_op jit(solution)/shard_map/ppermute | solution.py:23
  875.2 281.6 %collective-permute-start.25 = (bf16[512,16,48]{0,2,1:T(8,128)(2,1)}, bf16[512,16,48]{0,2,1:T(8,128)(2,1)}, u32[]{:S(2)}, u32[]{:S(2)}) collective-permute-start(bf16[512,16,48]{0,2,1:T(8,128)(2,1)} %select_convert_fusion.4), channel_id=1, source_target_pairs={{0,2},{1,3},{2,0},{3,1},{4,6},{5,7},{6,4},{7,5},{8,10},{9,11},{10,... | collective-permute-start | bytes 2359304 | tf_op jit(solution)/shard_map/ppermute | solution.py:23
  947.9 213.9 %collective-permute-start.27 = (bf16[512,16,48]{0,2,1:T(8,128)(2,1)}, bf16[512,16,48]{0,2,1:T(8,128)(2,1)}, u32[]{:S(2)}, u32[]{:S(2)}) collective-permute-start(bf16[512,16,48]{0,2,1:T(8,128)(2,1)} %select_convert_fusion.3), channel_id=1, source_target_pairs={{0,4},{1,5},{2,6},{3,7},{4,0},{5,1},{6,2},{7,3},{8,12},{9,13},{10,... | collective-permute-start | bytes 2359304 | tf_op jit(solution)/shard_map/ppermute | solution.py:23
  955.8 21.5 %copy-start.140 = (f32[512,16]{0,1:T(8,128)S(1)}, f32[512,16]{0,1:T(8,128)}, u32[]{:S(2)}) copy-start(f32[512,16]{0,1:T(8,128)} %get-tuple-element.1197) | copy-start | bytes 98308
  955.8 21.6 %copy-start.158 = (f32[16,16]{1,0:T(8,128)S(1)}, f32[16,16]{1,0:T(8,128)}, u32[]{:S(2)}) copy-start(f32[16,16]{1,0:T(8,128)} %copy.909) | copy-start | bytes 3076
  976.1 130.7 %collective-permute-start.30 = (bf16[256,16,48]{0,2,1:T(8,128)(2,1)}, bf16[256,16,48]{0,2,1:T(8,128)(2,1)}, u32[]{:S(2)}, u32[]{:S(2)}) collective-permute-start(bf16[256,16,48]{0,2,1:T(8,128)(2,1)} %select_convert_fusion.9), channel_id=1, source_target_pairs={{0,4},{1,5},{2,6},{3,7},{4,0},{5,1},{6,2},{7,3},{8,12},{9,13},{10,... | collective-permute-start | bytes 1179656 | tf_op jit(solution)/shard_map/ppermute | solution.py:23
  990.0 73.0 %collective-permute-start.33 = (bf16[128,16,48]{0,2,1:T(8,128)(2,1)}, bf16[128,16,48]{0,2,1:T(8,128)(2,1)}, u32[]{:S(2)}, u32[]{:S(2)}) collective-permute-start(bf16[128,16,48]{0,2,1:T(8,128)(2,1)} %select_convert_fusion.20), channel_id=1, source_target_pairs={{0,4},{1,5},{2,6},{3,7},{4,0},{5,1},{6,2},{7,3},{8,12},{9,13},{10,... | collective-permute-start | bytes 589832 | tf_op jit(solution)/shard_map/ppermute | solution.py:23
  1063.0 8.3 collective-permute-start.45
  1071.3 5.7 collective-permute-start.34
  1077.0 5.9 collective-permute-start.46
  1082.9 5.7 collective-permute-start.35
  1088.6 8.7 collective-permute-start.47
  1097.2 91.7 %collective-permute-start.36 = (bf16[512,16,48]{0,2,1:T(8,128)(2,1)}, bf16[512,16,48]{0,2,1:T(8,128)(2,1)}, u32[]{:S(2)}, u32[]{:S(2)}) collective-permute-start(bf16[512,16,48]{0,2,1:T(8,128)(2,1)} %select_convert_fusion.2), channel_id=1, source_target_pairs={{0,1},{1,0},{2,3},{3,2},{4,5},{5,4},{6,7},{7,6},{8,9},{9,8},{10,11... | collective-permute-start | bytes 2359304 | tf_op jit(solution)/shard_map/ppermute | solution.py:23
  1106.8 13.1 collective-permute-start.42
  1119.9 5.7 collective-permute-start.31
  1125.5 5.7 collective-permute-start.43
  1131.2 5.7 collective-permute-start.32
  1136.9 8.8 collective-permute-start.44
  1145.6 27.2 %collective-permute-start.37 = (bf16[512,16,48]{0,2,1:T(8,128)(2,1)}, bf16[512,16,48]{0,2,1:T(8,128)(2,1)}, u32[]{:S(2)}, u32[]{:S(2)}) collective-permute-start(bf16[512,16,48]{0,2,1:T(8,128)(2,1)} %select_convert_fusion.1), channel_id=1, source_target_pairs={{0,2},{1,3},{2,0},{3,1},{4,6},{5,7},{6,4},{7,5},{8,10},{9,11},{10,... | collective-permute-start | bytes 2359304 | tf_op jit(solution)/shard_map/ppermute | solution.py:23
  1156.8 27.6 %collective-permute-start.39 = (bf16[512,16,48]{0,2,1:T(8,128)(2,1)}, bf16[512,16,48]{0,2,1:T(8,128)(2,1)S(1)}, u32[]{:S(2)}, u32[]{:S(2)}) collective-permute-start(bf16[512,16,48]{0,2,1:T(8,128)(2,1)} %select_convert_fusion), channel_id=1, source_target_pairs={{0,4},{1,5},{2,6},{3,7},{4,0},{5,1},{6,2},{7,3},{8,12},{9,13},{10,... | collective-permute-start | bytes 2359304 | tf_op jit(solution)/shard_map/ppermute | solution.py:23
  1161.9 29.7 %collective-permute-start.26 = (bf16[256,16,48]{0,2,1:T(8,128)(2,1)S(1)}, bf16[256,16,48]{0,2,1:T(8,128)(2,1)S(1)}, u32[]{:S(2)}, u32[]{:S(2)}) collective-permute-start(bf16[256,16,48]{0,2,1:T(8,128)(2,1)S(1)} %select_convert_fusion.11), channel_id=1, source_target_pairs={{0,1},{1,0},{2,3},{3,2},{4,5},{5,4},{6,7},{7,6},{8,9},{9,8},{10,11... | collective-permute-start | bytes 1179656 | tf_op jit(solution)/shard_map/ppermute | solution.py:23
  1172.8 19.8 collective-permute-start.28
  1184.4 26.3 %collective-permute-start.38 = (bf16[256,16,48]{0,2,1:T(8,128)(2,1)}, bf16[256,16,48]{0,2,1:T(8,128)(2,1)}, u32[]{:S(2)}, u32[]{:S(2)}) collective-permute-start(bf16[256,16,48]{0,2,1:T(8,128)(2,1)} %select_convert_fusion.8), channel_id=1, source_target_pairs={{0,1},{1,0},{2,3},{3,2},{4,5},{5,4},{6,7},{7,6},{8,9},{9,8},{10,11... | collective-permute-start | bytes 1179656 | tf_op jit(solution)/shard_map/ppermute | solution.py:23
  1185.9 39.8 %collective-permute-start.40 = (bf16[256,16,48]{0,2,1:T(8,128)(2,1)S(1)}, bf16[256,16,48]{0,2,1:T(8,128)(2,1)}, u32[]{:S(2)}, u32[]{:S(2)}) collective-permute-start(bf16[256,16,48]{0,2,1:T(8,128)(2,1)S(1)} %select_convert_fusion.7), channel_id=1, source_target_pairs={{0,2},{1,3},{2,0},{3,1},{4,6},{5,7},{6,4},{7,5},{8,10},{9,11},{10,... | collective-permute-start | bytes 1179656 | tf_op jit(solution)/shard_map/ppermute | solution.py:23
  1209.6 18.4 collective-permute-start.29
  1227.0 10.2 collective-permute-start.41
  1336.5 678.8 %all-reduce.7.cloned.1.call-start = ((), (), s32[]{:S(2)}) async-start(), calls=%async_computation.4 | async-start | bytes 7090176
  (207 other events, 1377.1 us)
Sparse Core Ops, SparseCore 0:
  9.6 33.4 all-gather.8
  44.6 17.4 all-gather.10
  63.7 37.5 all-gather.12
  102.7 37.4 all-gather.14
  1336.6 246.3 all-reduce.8
  1877.5 137.7 all-reduce.6
where the time goes:
time: 2060 us; the launch traced here: 2040 us
  local copies, waits for them, and re-layouts  497 us (24%)
  waiting for transfers between devices  491 us (24%)
  matrix products  481 us (23%)
  blocking collectives  322 us (16%)
  other arithmetic  183 us (9%)
  starting transfers between devices  43.1 us (2%)
    unnamed x8, waiting for transfers between devices  373 us
    unnamed x1, blocking collectives  279 us
    mul x60, local copies, waits for them, and re-layouts, spread_rows(): grown_rows = tensor[:, None] * factors  161 us
    ppermute x48, waiting for transfers between devices, swapped(): lax.ppermute(array, axis, [(i, i ^ 1 << bit) for i in range(lax.axis_size...  118 us
    dot_general x31, matrix products, backward_block(): jnp.einsum('hqk,hqd->hkd', grad_scores, queries, preferred_element_type=j...  91.9 us
    dot_general x31, matrix products, backward_block(): jnp.einsum('hqk,hkd->hqd', grad_scores, key_block, preferred_element_type...  77.1 us
    dot_general x31, matrix products, backward_block(): jnp.einsum('hqd,hkd->hqk', grad_output, value_block, preferred_element_ty...  59.8 us
    dot_general x30, matrix products, backward_block(): jnp.einsum('hqd,hkd->hqk', queries, key_block, preferred_element_type=jnp...  50.8 us
  transfers between devices with their start and end apart: 54, of which 22 were waited for; matrix products, arithmetic and copies ran while one was open for 39% of the time, Pallas kernels for 0%

commit v1 on v0

v1 whole, which is shorter than its diff:
```python
import functools
import math

import jax
import jax.numpy as jnp
import ml_dtypes
import numpy as np
from jax import lax
from jax.experimental import pallas as pl
from jax.experimental.pallas import tpu as pltpu
from jax.sharding import PartitionSpec as P

HEADS = 16
HD = 48
D = HEADS * HD
SEG_BASE = 1024
BRANCHES = 5
T = 512
RES = 16
EPS = 1e-05
BIG = 2.0**100
SCALE = HD**-0.5
VMEM = 56 << 20
ORDER = np.array([int(f"{c:04b}"[::-1], 2) for c in range(RES)])
bf16, f32 = jnp.bfloat16, jnp.float32

VM = pl.BlockSpec(memory_space=pltpu.VMEM)
SM = pl.BlockSpec(memory_space=pltpu.SMEM)
HB = pl.BlockSpec(memory_space=pl.ANY)


def tdot(a, b):
    return lax.dot_general(a, b, (((0,), (0,)), ((), ())), preferred_element_type=f32)


def ndot(a, b):
    return lax.dot_general(a, b, (((1,), (0,)), ((), ())), preferred_element_type=f32)


def bdot(a, b):
    return lax.dot_general(a, b, (((1,), (1,)), ((), ())), preferred_element_type=f32)


def xdot(a, b):
    return lax.dot_general(a, b, (((0,), (1,)), ((), ())), preferred_element_type=f32)


def cost(us):
    return pl.CostEstimate(flops=int(us * 1e9), bytes_accessed=1000, transcendentals=0)


def kernel_call(body, in_specs, after=(), **kwargs):
    count = len(after)
    call = pl.pallas_call(
        (lambda *refs: body(*refs[count:])) if count else body,
        in_specs=[HB] * count + in_specs,
        compiler_params=pltpu.CompilerParams(vmem_limit_bytes=VMEM),
        **kwargs,
    )
    return functools.partial(call, *after)


def bit_reversed(h):
    return (h % 2) * 8 + (h // 2 % 2) * 4 + (h // 4 % 2) * 2 + h // 8


def split2(x):
    hi = x.astype(bf16)
    return hi, (x - hi.astype(f32)).astype(bf16)


def split3(x):
    a = x.astype(bf16).astype(f32)
    b = (x - a).astype(bf16).astype(f32)
    return a, b, x - a - b


def log_ratio(level):
    out = []
    for t in range(1, BRANCHES):
        c = math.log2((t + 1 - level) / (t - level)) if t > level else 0.0
        hi = float(np.asarray(c).astype(ml_dtypes.bfloat16))
        out.append((hi, float(np.asarray(c - hi).astype(ml_dtypes.bfloat16))))
    return out


def valuation(g, pos):
    c = pos >> 5
    hits = [((c >> n) == (g >> n)).astype(jnp.int32) for n in (3, 2, 1, 0)]
    return hits[0] + hits[1] + hits[2] + hits[3]


def query_side(g, q, docs, pos, level, lm=None):
    n = q.shape[1]
    hi, lo = split2(q.astype(f32) * (SCALE * math.log2(math.e)))
    row = lax.broadcasted_iota(jnp.int32, (32, n), 0)
    v = valuation(g, pos)
    f = jnp.where((row < 4) & (row == docs), -BIG, 0.0)
    for i, parts in enumerate(log_ratio(level)):
        for j, part in enumerate(parts):
            if part:
                f = jnp.where((row == 4 + 2 * i + j) & (v > i), part, f)
    if level >= 3:
        f = jnp.where(row == 12, -BIG, f)
    if level >= 4:
        f = jnp.where(row == 13, -BIG, f)
    if lm is not None:
        for r, part in enumerate(split3(lm)):
            f = jnp.where(row == 14 + r, -part, f)
    return jnp.concatenate([hi, lo, f.astype(bf16)], axis=0)


def key_side(g, k, docs):
    n = k.shape[1]
    pos = lax.broadcasted_iota(jnp.int32, (1, n), 1) & (T - 1)
    row = lax.broadcasted_iota(jnp.int32, (32, n), 0)
    v = valuation(g, pos)
    f = jnp.where((row < 4) & (row != docs), 1.0, 0.0)
    f = jnp.where((row >= 4) & (row < 12) & (v >= ((row - 2) >> 1)), 1.0, f)
    f = jnp.where((row == 12) & (v < 3), 1.0, f)
    f = jnp.where((row == 13) & (v < 4), 1.0, f)
    f = jnp.where((row >= 14) & (row < 17), 1.0, f)
    return jnp.concatenate([k, k, f.astype(bf16)], axis=0)


def ones_below(v, count):
    row = lax.broadcasted_iota(jnp.int32, (16, v.shape[1]), 0)
    return jnp.concatenate([v, jnp.where(row < count, 1.0, 0.0).astype(bf16)], axis=0)


def positions(first, n, width):
    return first + (lax.broadcasted_iota(jnp.int32, (1, n), 1) & (width - 1))


def attend(jobs):
    scores = [tdot(kf, qf) for kf, _, qf in jobs]
    tops = [jnp.max(s, axis=0, keepdims=True) for s in scores]
    weights = [jnp.exp2(s - m).astype(bf16) for s, m in zip(scores, tops)]
    outs = [ndot(v1, p) for (_, v1, _), p in zip(jobs, weights)]
    return [(o[:HD] * (1.0 / o[HD : HD + 1]), m + jnp.log2(o[HD : HD + 1])) for o, m in zip(outs, tops)]


def attend_back(jobs):
    weights = [jnp.exp2(tdot(kf, qf)) for kf, _, _, qf, _, _ in jobs]
    slopes = [tdot(v3, gf) for _, _, v3, _, _, gf in jobs]
    ds = [(p * dp).astype(bf16) for p, dp in zip(weights, slopes)]
    ps = [p.astype(bf16) for p in weights]
    return [(ndot(k, d), bdot(q, d), bdot(gf[:HD], p)) for (_, k, _, _, q, gf), d, p in zip(jobs, ds, ps)]


def gradient_side(grad, dd):
    row = lax.broadcasted_iota(jnp.int32, (16, grad.shape[1]), 0)
    f = jnp.zeros((16, grad.shape[1]), f32)
    for r, part in enumerate(split3(dd)):
        f = jnp.where(row == r, -part, f)
    return jnp.concatenate([grad, f.astype(bf16)], axis=0)


TILE = 256
TILES = [slice(at, at + TILE) for at in range(0, T, TILE)]


def head_of(ref, i, rows=HD):
    return ref[i * rows : (i + 1) * rows]


def near_kernel(q_ref, k_ref, v_ref, docs_ref, o_ref, lm_ref):
    docs = docs_ref[...]
    jobs = []
    for i in range(NEAR):
        g = pl.program_id(0) * NEAR + i
        kf = key_side(g, head_of(k_ref, i), docs)
        v1 = ones_below(head_of(v_ref, i), 1)
        q = head_of(q_ref, i)
        jobs += [(kf, v1, query_side(g, q[:, c], docs[:, c], positions(c.start, TILE, T), 0)) for c in TILES]
    done = attend(jobs)
    for i in range(NEAR):
        for c in TILES:
            o, lm = done.pop(0)
            o_ref[i * HD : (i + 1) * HD, c] = o
            lm_ref[i, :, c] = lm


def window(ref, g, level):
    w = T >> min(level, 2)
    at = pl.multiple_of((g >> (4 - min(level, 2))) * w, 128)
    return jnp.concatenate([ref[:, pl.ds(at, w)], ref[:, pl.ds(T + at, w)]], axis=1)


def guest_side(g, level, q, docs_ref, lm=None):
    width = T >> level
    block = g >> (4 - level)
    rows = docs_ref[...].astype(f32)
    pick = lax.broadcasted_iota(jnp.int32, rows.shape, 0) == block
    docs = jnp.sum(jnp.where(pick, rows, 0.0), axis=0, keepdims=True).astype(jnp.int32)
    return query_side(g, q, docs, positions(block * width, q.shape[1], width), level, lm)


def stat_rows(rows):
    parts = [p for row in rows for p in split3(row)]
    return jnp.concatenate(parts + [jnp.zeros((16 - len(parts), rows[0].shape[1]), f32)], axis=0).astype(bf16)


def stat_row(block, i):
    rows = block[HD + 3 * i : HD + 3 * i + 3].astype(f32)
    return rows[0:1] + rows[1:2] + rows[2:3]


def far_kernel(levels, k_ref, v_ref, docs_ref, *refs):
    kf_ref = refs[-1]
    ins, outs = refs[: 2 * len(levels)], refs[2 * len(levels) : -1]
    jobs = []
    for i in range(FAR):
        g = pl.program_id(0) * FAR + i
        kf_ref[i] = key_side(g, head_of(k_ref, i), docs_ref[...])
        rows = pl.ds(i * HD, HD)
        for j, level in enumerate(levels):
            qf = guest_side(g, level, head_of(ins[2 * j], i), ins[2 * j + 1])
            jobs.append((window(kf_ref.at[i], g, level), ones_below(window(v_ref.at[rows], g, level), 1), qf))
    done = attend(jobs)
    for i in range(FAR):
        for out in outs:
            o, lm = done.pop(0)
            out[i * ROWS : (i + 1) * ROWS] = jnp.concatenate([o.astype(bf16), stat_rows([lm])], axis=0)


def near_back_kernel(first, q_ref, k_ref, v_ref, docs_ref, g_ref, lm_ref, dd_ref, *refs):
    gq_ref, gk_ref, gv_ref = refs[-3:]
    docs = docs_ref[...]
    jobs = []
    for i in range(NEAR):
        g = pl.program_id(0) * NEAR + i + first
        k, q, grad, lm, dd = head_of(k_ref, i), head_of(q_ref, i), head_of(g_ref, i), lm_ref[i], dd_ref[i]
        kf = key_side(g, k, docs)
        v3 = ones_below(head_of(v_ref, i), 3)
        for c in TILES:
            qf = query_side(g, q[:, c], docs[:, c], positions(c.start, TILE, T), 0, lm[:, c])
            jobs.append((kf, k, v3, qf, q[:, c], gradient_side(grad[:, c], dd[:, c])))
    done = attend_back(jobs)
    for i in range(NEAR):
        rows = slice(i * HD, (i + 1) * HD)
        mine = [done.pop(0) for _ in TILES]
        for c, (dq, _, _) in zip(TILES, mine):
            gq_ref[rows, c] = (dq * SCALE).astype(bf16)
        gk_ref[rows] = (sum(d[1] for d in mine) * SCALE).astype(bf16)
        gv_ref[rows] = sum(d[2] for d in mine).astype(bf16)


def far_back_kernel(levels, k_ref, v_ref, docs_ref, *refs):
    kf_ref, ak_ref, av_ref = refs[-3:]
    n = len(levels)
    ins, outs = refs[: 3 * n], refs[3 * n : -3]
    jobs = []
    for i in range(FAR):
        g = pl.program_id(0) * FAR + i
        kf_ref[i] = key_side(g, head_of(k_ref, i), docs_ref[...])
        rows = pl.ds(i * HD, HD)
        for j, level in enumerate(levels):
            q_ref, dq_ref, g_ref = ins[3 * j : 3 * j + 3]
            q, grad = head_of(q_ref, i), head_of(g_ref, i, ROWS)
            qf = guest_side(g, level, q, dq_ref, stat_row(grad, 0))
            gf = gradient_side(grad[:HD], stat_row(grad, 1))
            k, v = window(k_ref.at[rows], g, level), window(v_ref.at[rows], g, level)
            jobs.append((window(kf_ref.at[i], g, level), k, ones_below(v, 3), qf, q, gf))
    done = attend_back(jobs)
    ak_ref[...] = jnp.zeros_like(ak_ref)
    av_ref[...] = jnp.zeros_like(av_ref)
    for i in range(FAR):
        g = pl.program_id(0) * FAR + i
        rows = slice(i * HD, (i + 1) * HD)
        for j, level in enumerate(levels):
            dq, dk, dv = done.pop(0)
            outs[2 + j][rows] = (dq * SCALE).astype(bf16)
            w = T >> min(level, 2)
            at = (g >> (4 - min(level, 2))) * w
            for c in range(2):
                cols = pl.ds(pl.multiple_of(c * T + at, 128), w)
                ak_ref[rows, cols] += dk[:, c * w : (c + 1) * w]
                av_ref[rows, cols] += dv[:, c * w : (c + 1) * w]
    outs[0][...] = (ak_ref[...] * SCALE).astype(bf16)
    outs[1][...] = av_ref[...].astype(bf16)


NEAR, FAR = 2, 4
ROWS = 64


def head_rows(n, heads, first=0, rows=HD):
    return pl.BlockSpec((rows * heads, n), lambda i: (i + first // heads, 0))


def head_stats(n, heads, first=0):
    return pl.BlockSpec((heads, 1, n), lambda i: (i + first // heads, 0, 0))


def whole(*shape):
    return pl.BlockSpec(shape, lambda i: (0,) * len(shape))


def guest_docs(n):
    return pl.BlockSpec((16, n), lambda i: (D // 16, 0))


def shape_of(*dims, dtype=bf16):
    return jax.ShapeDtypeStruct(dims, dtype)


def attend_near(q, k, v, docs):
    r = lambda n: head_rows(n, NEAR)
    return kernel_call(
        near_kernel,
        grid=(HEADS // NEAR,),
        in_specs=[r(T), r(2 * T), r(2 * T), whole(1, 2 * T)],
        out_specs=[r(T), head_stats(T, NEAR)],
        out_shape=[shape_of(D, T, dtype=f32), shape_of(HEADS, 1, T, dtype=f32)],
        cost_estimate=cost(1),
        name="near",
    )(q, k, v, docs)


def attend_far(k, v, docs, guests, after):
    r = lambda n: head_rows(n, FAR)
    in_specs = [r(2 * T), r(2 * T), whole(1, 2 * T)]
    out_specs, out_shape, args = [], [], []
    for level, q in guests:
        n = q.shape[1]
        in_specs += [r(n), guest_docs(n)]
        out_specs.append(head_rows(n, FAR, 0, ROWS))
        out_shape.append(shape_of(ROWS * HEADS, n))
        args += [q, q]
    return kernel_call(
        functools.partial(far_kernel, [v[0] for v in guests]),
        after=after,
        grid=(HEADS // FAR,),
        in_specs=in_specs,
        out_specs=out_specs,
        out_shape=out_shape,
        scratch_shapes=[pltpu.VMEM((FAR, 128, 2 * T), bf16)],
        cost_estimate=cost(1),
        name="far",
    )(k, v, docs, *args)


def near_back(q, k, v, docs, grads, lm, dd, first, count, rest=(), after=()):
    r = lambda n: head_rows(n, NEAR, first)
    return kernel_call(
        functools.partial(near_back_kernel, first),
        after=after,
        grid=(count // NEAR,),
        in_specs=[r(T), r(2 * T), r(2 * T), whole(1, 2 * T), r(T), head_stats(T, NEAR, first), head_stats(T, NEAR, first)] + [HB] * len(rest),
        out_specs=[r(T), r(2 * T), r(2 * T)],
        out_shape=[shape_of(D, n) for n in (T, 2 * T, 2 * T)],
        input_output_aliases={len(after) + 7 + i: i for i in range(len(rest))},
        cost_estimate=cost(1),
        name="near_back",
    )(q, k, v, docs, grads, lm, dd, *rest)


def far_back(k, v, docs, guests, after):
    r = lambda n: head_rows(n, FAR)
    in_specs = [r(2 * T), r(2 * T), whole(1, 2 * T)]
    out_specs, out_shape, args = [r(2 * T)] * 2, [shape_of(D, 2 * T)] * 2, []
    for level, q, grads in guests:
        n = q.shape[1]
        in_specs += [r(n), guest_docs(n), head_rows(n, FAR, 0, ROWS)]
        out_specs.append(r(n))
        out_shape.append(shape_of(D, n))
        args += [q, q, grads]
    return kernel_call(
        functools.partial(far_back_kernel, [v[0] for v in guests]),
        after=after,
        grid=(HEADS // FAR,),
        in_specs=in_specs,
        out_specs=out_specs,
        out_shape=out_shape,
        scratch_shapes=[pltpu.VMEM((FAR, 128, 2 * T), bf16), pltpu.VMEM((FAR * HD, 2 * T), f32), pltpu.VMEM((FAR * HD, 2 * T), f32)],
        cost_estimate=cost(1),
        name="far_back",
    )(k, v, docs, *args)


def permutation():
    p = lax.broadcasted_iota(jnp.int32, (T, T), 0)
    o = lax.broadcasted_iota(jnp.int32, (T, T), 1)
    return jnp.where(o == p % 32 * RES + bit_reversed(p // 32), 1.0, 0.0).astype(bf16)


def normalized(x):
    center = jnp.mean(x, axis=-1, keepdims=True)
    centered = x - center
    rstd = lax.rsqrt(jnp.mean(centered * centered, axis=-1, keepdims=True) + EPS)
    return centered * rstd, rstd


def norm_pullback(grad, xhat, rstd, gain):
    g = grad * gain
    gx = rstd * (g - jnp.mean(g, axis=-1, keepdims=True) - xhat * jnp.mean(g * xhat, axis=-1, keepdims=True))
    return gx, jnp.sum(grad * xhat, axis=0, keepdims=True), jnp.sum(grad, axis=0, keepdims=True)


def fetch(shards, buffer, sems, where_ref, rows):
    out = []
    for r, shard in enumerate(shards):
        at = pl.multiple_of(where_ref[r] * rows, rows)
        out.append(pltpu.make_async_copy(shard.at[pl.ds(0, rows)], buffer.at[pl.ds(at, rows)], sems.at[r]))
        out[-1].start()
    return out


def add_bias(values, row_ref, r):
    pick = jnp.where(lax.broadcasted_iota(jnp.int32, (16, values.shape[1]), 0) == r, 1.0, 0.0).astype(bf16)
    return values + tdot(row_ref, pick)


def block_lanes(g, level):
    at = g // (RES >> level) * (T >> level)
    return slice(at, at + (T >> level))


def head_slice(g):
    return slice(g * HD, (g + 1) * HD)


def project_kernel(levels, where_ref, w0, w1, w2, w3, vec_ref, bias_ref, docs_ref, x0_ref, x1_ref, *refs):
    q_ref, k_ref, v_ref, n_ref, in_ref, dout_ref = refs[:6]
    visit_refs = refs[6 : 5 + levels]
    w_ref, wt_ref, sems = refs[5 + levels :]
    copies = fetch((w0, w1, w2, w3), w_ref, sems, where_ref, D // 4)
    perm = permutation()
    gain, shift = vec_ref[0:1], vec_ref[2:3]

    def norm(x):
        xhat, _ = normalized(x.astype(f32))
        return ndot(perm, (xhat * gain + shift).astype(bf16)).astype(bf16)

    in_ref[...] = ndot(perm, x0_ref[...]).astype(bf16)
    n_ref[:T] = norm(x0_ref[...])
    n_ref[T:] = norm(x1_ref[:T])
    own_docs = bdot(jnp.broadcast_to(docs_ref[...].astype(f32), (8, T)).astype(bf16), perm)[0:1]
    near_docs = bdot(x1_ref[T:, :T], perm)[0:1]
    dout_ref[...] = jnp.concatenate([own_docs, near_docs], axis=1).astype(jnp.int32)
    for c in copies:
        c.wait()
    for part in range(3):
        wt = w_ref[:, part * D : (part + 1) * D].T
        for g in range(HEADS):
            h = int(ORDER[g])
            wt_ref[part * D + g * HD : part * D + (g + 1) * HD, :] = wt[head_slice(h)]
    n = n_ref[...]
    q_ref[...] = add_bias(bdot(wt_ref[:D, :], n_ref[:T]), bias_ref[...], 0).astype(bf16)
    for level in range(1, levels):
        width = T >> level
        visit = visit_refs[level - 1]
        for g in range(HEADS):
            visit[head_slice(g), :] = q_ref[head_slice(g), block_lanes(g, level)]
        rows = [own_docs[:, b * width : (b + 1) * width] for b in range(1 << level)]
        if level < 4:
            rows.append(jnp.zeros((16 - len(rows), width), f32))
        visit[D:, :] = jnp.concatenate(rows, axis=0).astype(bf16)
    k_ref[...] = bdot(wt_ref[D : 2 * D, :], n).astype(bf16)
    v_ref[...] = add_bias(bdot(wt_ref[2 * D :, :], n), bias_ref[...], 1).astype(bf16)


def project(levels, where, shards, vectors, biases, docs, tile, tile_near):
    return kernel_call(
        functools.partial(project_kernel, levels),
        in_specs=[SM] + [HB] * 4 + [VM] * 5,
        out_specs=[VM] * (5 + levels),
        out_shape=[shape_of(D, T), shape_of(D, 2 * T), shape_of(D, 2 * T), shape_of(2 * T, D), shape_of(T, D), shape_of(1, 2 * T, dtype=jnp.int32)]
        + [shape_of(D + 16, T >> level) for level in range(1, levels)],
        scratch_shapes=[pltpu.VMEM((D, 3 * D), bf16), pltpu.VMEM((3 * D, D), bf16), pltpu.SemaphoreType.DMA((4,))],
        cost_estimate=cost(1),
        name="project",
    )(where, *shards, vectors, biases, docs, tile, tile_near)


ERF_TOP = (0.00022905065861350646, 0.0034082910107109506, 0.050955695062380861, 0.18520832239976145, 1.128379143519084)
ERF_BOTTOM = (-1.1791602954361697e-7, 0.000023547966471313185, 0.0010179625278914885, 0.014070470171167667, 0.11098505178285362, 0.49746925110067538, 1.0)


def erf(x):
    x = jnp.clip(x, -3.7439211627767994, 3.7439211627767994)
    y = x * x
    top, bottom = ERF_TOP[0], ERF_BOTTOM[0]
    for c in ERF_TOP[1:]:
        top = top * y + c
    for c in ERF_BOTTOM[1:]:
        bottom = bottom * y + c
    return x * top / bottom


FF_PART = 768
FF_ROWS = 2 * FF_PART + D // 4


def merge_heads(o_ref, lm_ref, back, merged_ref, lmf_ref):
    for g in range(HEADS):
        base = lm_ref[g]
        parts, top = [], base
        blocks = [head_of(ref, g, ROWS) for _, ref in back]
        for (level, _), block in zip(back, blocks):
            cols = block_lanes(g, level)
            rest = [jnp.full((1, n), -BIG, f32) for n in (cols.start, T - cols.stop)]
            parts.append(jnp.concatenate([x for x in (rest[0], stat_row(block, 0), rest[1]) if x.shape[1]], axis=1))
            top = jnp.maximum(top, parts[-1])
        weights = [jnp.exp2(x - top) for x in [base] + parts]
        total = sum(weights)
        scale = 1.0 / total
        out = o_ref[head_slice(g), :] * (weights[0] * scale)
        for (level, _), block, w in zip(back, blocks, weights[1:]):
            cols = block_lanes(g, level)
            add = block[:HD].astype(f32) * (w * scale)[:, cols]
            rest = [jnp.zeros((HD, n), f32) for n in (cols.start, T - cols.stop)]
            out = out + jnp.concatenate([x for x in (rest[0], add, rest[1]) if x.shape[1]], axis=1)
        merged_ref[head_slice(int(ORDER[g])), :] = out
        lmf_ref[g] = top + jnp.log2(total)


def middle_kernel(levels, back_levels, where_ref, *refs):
    shards, refs = refs[:4], refs[4:]
    o_ref, lm_ref, in_ref, cot_ref, vec_ref, hb_ref = refs[:6]
    n = len(back_levels)
    back = list(zip(back_levels, refs[6 : 6 + n]))
    refs = refs[6 + n :]
    enc_ref, mine_out, theirs_out, gm_ref, dd_ref, lmf_ref, gmid_ref, small_ref, gbias_ref = refs[:9]
    grad_out = lambda r, at, rows: (mine_out, theirs_out)[r % 2].at[r // 2, pl.ds(at, rows)]
    visit_refs, refs = refs[9 : 8 + levels], refs[8 + levels :]
    wo_ref, wu_ref, wd_ref, gd_ref, gu_ref, act_ref, merged_ref, y_ref, gn_ref, gy_ref, n2_ref, sems, osems = refs
    out_copies = fetch(shards, wo_ref, sems.at[0], where_ref, D // 4)
    up_copies, down_copies = [], []
    for r, shard in enumerate(shards):
        rows = pl.ds(pl.multiple_of(where_ref[r] * (D // 4), D // 4), D // 4)
        for c in range(4):
            dst = wu_ref.at[rows, pl.ds(c * FF_PART, FF_PART)]
            up_copies.append(pltpu.make_async_copy(shard.at[pl.ds((1 + c) * (D // 4), D // 4)], dst, sems.at[1 + c, r]))
            up_copies[-1].start()
    for r, shard in enumerate(shards):
        down_copies.append(pltpu.make_async_copy(shard.at[pl.ds(5 * (D // 4), FF_PART)], wd_ref.at[r], sems.at[5, r]))
        down_copies[-1].start()
    perm = permutation()
    gy_ref[...] = ndot(perm, cot_ref[...]).astype(bf16)
    merge_heads(o_ref, lm_ref, back, merged_ref, lmf_ref)
    merged = merged_ref[...].astype(bf16)
    for c in out_copies:
        c.wait()
    middle = in_ref[...].astype(f32) + tdot(merged, wo_ref[...]) + vec_ref[5:6]
    xhat, rstd = normalized(middle)
    n2_ref[...] = (xhat * vec_ref[1:2] + vec_ref[6:7]).astype(bf16)
    y_ref[...] = middle + vec_ref[7:8]
    gn_ref[...] = jnp.zeros_like(gn_ref)
    for c in up_copies:
        c.wait()
    down_parts = []
    for r in range(4):
        at = pl.multiple_of(where_ref[r] * FF_PART, FF_PART)
        cols = pl.ds(at, FF_PART)
        down_copies[r].wait()
        n2, gy = n2_ref[...], gy_ref[...]
        hidden = ndot(n2, wu_ref[:, cols]) + hb_ref[:, cols]
        phi = 0.5 + 0.5 * erf(hidden * 0.5**0.5)
        slope = phi + hidden * (jnp.exp(hidden * hidden * -0.5) * (2 * math.pi) ** -0.5)
        active = (hidden * phi).astype(bf16)
        y_ref[...] += ndot(active, wd_ref[r])
        gd_ref[r] = tdot(active, gy).astype(bf16)
        down_parts.append(pltpu.make_async_copy(gd_ref.at[r], grad_out(r, 0, FF_PART), osems.at[r]))
        down_parts[-1].start()
        gh = (slope * bdot(gy, wd_ref[r])).astype(bf16)
        gbias_ref[:, cols] = jnp.sum(gh.astype(f32), axis=0, keepdims=True)
        gu_ref[:, cols] = tdot(n2, gh).astype(bf16)
        gn_ref[...] += bdot(gh, wu_ref[:, cols])
    up_parts = []
    for r in range(4):
        at = pl.multiple_of(where_ref[r] * (D // 4), D // 4)
        for c in range(4):
            src = gu_ref.at[pl.ds(at, D // 4), pl.ds(c * FF_PART, FF_PART)]
            up_parts.append(pltpu.make_async_copy(src, grad_out(r, FF_PART + (1 + c) * (D // 4), D // 4), osems.at[8 + 4 * r + c]))
            up_parts[-1].start()
    enc_ref[...] = tdot(perm, y_ref[...].astype(bf16)).astype(bf16)
    gy = gy_ref[...].astype(f32)
    middle = in_ref[...].astype(f32) + tdot(merged, wo_ref[...]) + vec_ref[5:6]
    xhat, rstd = normalized(middle)
    gx, ggain, gshift = norm_pullback(gn_ref[...], xhat, rstd, vec_ref[1:2])
    gmid = gy + gx
    gmid_ref[...] = gmid
    gatt = gmid.astype(bf16)
    act_ref[...] = ndot(merged, gatt).astype(bf16)
    for r in range(4):
        at = pl.multiple_of(where_ref[r] * (D // 4), D // 4)
        down_parts.append(pltpu.make_async_copy(act_ref.at[pl.ds(at, D // 4)], grad_out(r, FF_PART, D // 4), osems.at[4 + r]))
        down_parts[-1].start()
    gm = bdot(wo_ref[...], gatt)
    prod = gm * merged_ref[...]
    gm = gm.astype(bf16)
    for g in range(HEADS):
        h = head_slice(int(ORDER[g]))
        gm_ref[head_slice(g), :] = gm[h]
        dd = jnp.sum(prod[h], axis=0, keepdims=True)
        dd_ref[g] = dd
        for level in range(1, levels):
            cols = block_lanes(g, level)
            block = jnp.concatenate([gm[h, cols], stat_rows([lmf_ref[g][:, cols], dd[:, cols]])], axis=0)
            visit_refs[level - 1][g * ROWS : (g + 1) * ROWS] = block
    zero = jnp.zeros((4, D), f32)
    small_ref[...] = jnp.concatenate(
        [ggain, jnp.sum(gatt.astype(f32), axis=0, keepdims=True), gshift, jnp.sum(gy, axis=0, keepdims=True), zero], axis=0)
    for c in down_parts + up_parts:
        c.wait()


def middle(levels, where, shards, o, lm, back, inputs, cotangent, vectors, bias):
    s = shape_of
    ff = bias.shape[1]
    visits = [s(ROWS * HEADS, T >> level) for level in range(1, levels)]
    return kernel_call(
        functools.partial(middle_kernel, levels, [b[0] for b in back]),
        in_specs=[SM] + [HB] * 4 + [VM] * (6 + len(back)),
        out_specs=[VM] + [HB] * 2 + [VM] * (6 + len(visits)),
        out_shape=[
            s(T, D), s(2, FF_ROWS, D), s(2, FF_ROWS, D),
            s(D, T), s(HEADS, 1, T, dtype=f32), s(HEADS, 1, T, dtype=f32), s(T, D, dtype=f32), s(8, D, dtype=f32), s(1, ff, dtype=f32),
        ] + visits,
        scratch_shapes=[
            pltpu.VMEM((D, D), bf16), pltpu.VMEM((D, ff), bf16), pltpu.VMEM((4, FF_PART, D), bf16),
            pltpu.VMEM((4, FF_PART, D), bf16), pltpu.VMEM((D, ff), bf16), pltpu.VMEM((D, D), bf16), pltpu.VMEM((D, T), f32),
            pltpu.VMEM((T, D), f32), pltpu.VMEM((T, D), f32), pltpu.VMEM((T, D), bf16), pltpu.VMEM((T, D), bf16),
            pltpu.SemaphoreType.DMA((6, 4)), pltpu.SemaphoreType.DMA((24,)),
        ],
        cost_estimate=cost(1),
        name="middle",
    )(where, *shards, o, lm, inputs, cotangent, vectors, bias, *[b[1] for b in back])


def natural(refs):
    rows = []
    for h in range(HEADS):
        g = head_slice(int(ORDER[h]))
        rows.append(sum(ref[g, :].astype(f32) for ref in refs).astype(bf16))
    return jnp.concatenate(rows, axis=0)


def to_blocks(where_ref, src_ref, out_refs, parts):
    rows = D // 4
    for r in range(4):
        at = pl.multiple_of(where_ref[r] * rows, rows)
        for part in range(parts):
            out_refs[r % 2][r // 2, part * rows : (part + 1) * rows, :] = src_ref[pl.ds(at, rows), part * D : (part + 1) * D]


def keys_kernel(where_ref, w0, w1, w2, w3, nk_ref, nv_ref, fk_ref, fv_ref, n_ref,
                send_ref, own_ref, mine_ref, theirs_ref, sums_ref, w_ref, gp_ref, gw_ref, sems):
    copies = fetch((w0, w1, w2, w3), w_ref, sems, where_ref, D // 4)
    gp_ref[:D] = natural((nk_ref, fk_ref))
    gp_ref[D:] = natural((nv_ref, fv_ref))
    for c in copies:
        c.wait()
    send_ref[...] = xdot(gp_ref[:, T:], w_ref[:, D:]).astype(bf16)
    gw_ref[...] = xdot(n_ref[...], gp_ref[...]).astype(bf16)
    to_blocks(where_ref, gw_ref, (mine_ref, theirs_ref), 2)
    own_ref[...] = xdot(gp_ref[:, :T], w_ref[:, D:])
    sums_ref[...] = bdot(jnp.ones((16, 2 * T), bf16), gp_ref[D:, :])[:8]


def keys_last(where, shards, grads, normed, after):
    s = shape_of
    return kernel_call(
        keys_kernel,
        after=after,
        in_specs=[SM] + [HB] * 4 + [VM] * 5,
        out_specs=[VM] * 5,
        out_shape=[s(T, D), s(T, D, dtype=f32), s(2, D // 2, D), s(2, D // 2, D), s(8, D, dtype=f32)],
        scratch_shapes=[pltpu.VMEM((D, 3 * D), bf16), pltpu.VMEM((2 * D, 2 * T), bf16), pltpu.VMEM((D, 2 * D), bf16), pltpu.SemaphoreType.DMA((4,))],
        cost_estimate=cost(1),
        name="keys_last",
    )(where, *shards, *grads, normed)


LAST_ROWS = 256


def last_kernel(back_levels, where_ref, w0, w1, w2, w3, gq_ref, *refs):
    back = list(zip(back_levels, refs))
    n_ref, in_ref, gmid_ref, vec_ref, small_ref, gbias_ref, own_ref, got_ref, sums_ref, gt_ref, mine_ref, theirs_ref = refs[len(back) : len(back) + 12]
    w_ref, gp_ref, gw_ref, sems = refs[len(back) + 12 :]
    copies = fetch((w0, w1, w2, w3), w_ref, sems, where_ref, D // 4)
    for g in range(HEADS):
        rows = head_slice(g)
        total = gq_ref[rows, :].astype(f32)
        for level, ref in back:
            cols = block_lanes(g, level)
            rest = [jnp.zeros((HD, n), f32) for n in (cols.start, T - cols.stop)]
            total = total + jnp.concatenate([x for x in (rest[0], ref[rows, :].astype(f32), rest[1]) if x.shape[1]], axis=1)
        gp_ref[head_slice(int(ORDER[g])), :] = total.astype(bf16)
    gw_ref[...] = xdot(n_ref[:T], gp_ref[...]).astype(bf16)
    to_blocks(where_ref, gw_ref, (mine_ref, theirs_ref), 1)
    sums = bdot(jnp.ones((16, T), bf16), gp_ref[...])
    for c in copies:
        c.wait()
    grad = xdot(gp_ref[...], w_ref[:, :D]) + own_ref[...] + got_ref[...].astype(f32)
    xhat, rstd = normalized(in_ref[...].astype(f32))
    gx, ggain, gshift = norm_pullback(grad, xhat, rstd, vec_ref[0:1])
    rows = [ggain, small_ref[0:1], gshift, sums[0:1], sums_ref[0:1], small_ref[1:4]]
    rows += [gbias_ref[:, i * D : (i + 1) * D] for i in range(4)]
    rows += [jnp.zeros((4, D), f32)]
    small = jnp.concatenate(rows, axis=0).astype(bf16)
    for out in (mine_ref, theirs_ref):
        for r in range(2):
            out[r, D // 4 : D // 4 + 16, :] = small
            out[r, D // 4 + 16 :, :] = jnp.zeros((LAST_ROWS - D // 4 - 16, D), bf16)
    gt_ref[...] = tdot(permutation(), (gmid_ref[...] + gx).astype(bf16)).astype(bf16)


def last(where, shards, gq, back, normed, inputs, gmid, vectors, small, gbias, own, got, sums, after):
    return kernel_call(
        functools.partial(last_kernel, [b[0] for b in back]),
        after=after,
        in_specs=[SM] + [HB] * 4 + [VM] * (10 + len(back)),
        out_specs=[VM] * 3,
        out_shape=[shape_of(T, D), shape_of(2, LAST_ROWS, D), shape_of(2, LAST_ROWS, D)],
        scratch_shapes=[pltpu.VMEM((D, 3 * D), bf16), pltpu.VMEM((D, T), bf16), pltpu.VMEM((D, D), bf16), pltpu.SemaphoreType.DMA((4,))],
        cost_estimate=cost(1),
        name="last",
    )(where, *shards, gq, *[b[1] for b in back], normed, inputs, gmid, vectors, small, gbias, own, got, sums)


def exchanged(x, axis, mask):
    return lax.ppermute(x, axis, [(i, i ^ mask) for i in range(lax.axis_size(axis))])


def added(a, b):
    return (a.astype(f32) + b.astype(f32)).astype(bf16)


def behind(x, other):
    return lax.optimization_barrier((x, other))[0]


def core_sum(mine, theirs):
    return added(mine, exchanged(theirs, "fsdp", 1))


def halved(x, rank, bit):
    half = x.shape[1] // 2
    mine = rank >> bit & 1
    kept = lax.dynamic_slice_in_dim(x, mine * half, half, 1)
    sent = lax.dynamic_slice_in_dim(x, (1 - mine) * half, half, 1)
    return added(kept, exchanged(sent, "seq", 1 << bit))


def doubled(x, rank, bit):
    theirs = exchanged(x, "seq", 1 << bit)
    low = (rank >> bit & 1) == 0
    return jnp.concatenate([jnp.where(low, x, theirs), jnp.where(low, theirs, x)], axis=1)


def chip_sum(x):
    return added(x[:1], exchanged(x[1:], "fsdp", 2))


def beyond(x, seq):
    for bit in range(3, seq.bit_length() - 1):
        x = added(x, exchanged(x, "seq", 1 << bit))
    return x


def direct(mine, theirs, seq):
    pair = core_sum(mine, theirs)
    own = added(pair[0], exchanged(pair[1], "fsdp", 2))
    pieces = lax.all_to_all(own.reshape(seq, -1, D), "seq", 0, 0)
    piece = jnp.sum(pieces.astype(f32), axis=0).astype(bf16)
    return lax.all_to_all(jnp.broadcast_to(piece[None], (seq,) + piece.shape), "seq", 0, 0).reshape(-1, D)


def local(tiles, documents, cotangent, w_qkv, w_out, w_up, w_down, gains, shifts, hidden_bias):
    seq = lax.axis_size("seq")
    rank = lax.axis_index("seq")
    part = lax.axis_index("fsdp")
    levels = min(BRANCHES, (seq * T // SEG_BASE).bit_length())
    where = jnp.stack([part ^ r for r in range(4)]).astype(jnp.int32)
    visits = [(level, (1 << level) + 2 * c) for level in range(1, levels) for c in range(1 << level - 1)]
    cols = gains.shape[1]

    packed = jnp.concatenate([gains, shifts, hidden_bias.reshape(-1, cols)], axis=0).reshape(1, -1)
    w_ext = jnp.concatenate([w_qkv, jnp.pad(packed, ((0, 7), (0, 0)))], axis=0)
    qkv_far = exchanged(w_ext, "fsdp", 2)
    tile = tiles[0]
    docs_row = jnp.pad(documents.astype(bf16), ((0, 7), (0, D - T)))
    tile_near = exchanged(jnp.concatenate([tile, docs_row], axis=0), "seq", 1)
    stacked_up = w_up.reshape(cols, -1, D).swapaxes(0, 1).reshape(-1, D)
    w_ff = jnp.concatenate([w_out, stacked_up, w_down], axis=0)
    ff_far = exchanged(w_ff, "fsdp", 2)
    qkv_near = exchanged(w_ext, "fsdp", 1)
    qkv_shards = (w_ext, qkv_near, qkv_far, exchanged(behind(qkv_far, tile_near), "fsdp", 1))
    ff_near = exchanged(w_ff, "fsdp", 1)

    stacked = jnp.stack([w[cols].reshape(-1, cols) for w in qkv_shards])
    in_order = jnp.stack([lax.dynamic_index_in_dim(stacked, part ^ s, 0, keepdims=False) for s in range(4)])
    rows = in_order[:, :8].transpose(1, 0, 2).reshape(8, D)
    vectors = rows.astype(f32)
    bias_row = in_order[:, 8:].reshape(1, -1).astype(f32)
    by_head = rows[3:5].reshape(2, 2, 2, 2, 2, HD).transpose(0, 4, 3, 2, 1, 5).reshape(2, D)
    biases = jnp.concatenate([by_head, jnp.zeros((14, D), bf16)], axis=0)

    q, k, v, normed, inputs, docs, *queries = project(levels, where, qkv_shards, vectors, biases, documents, tile, tile_near)
    guests = [(level, exchanged(queries[level - 1], "seq", mask)) for level, mask in visits]
    o, lm = attend_near(q, k, v, docs)
    partial = attend_far(k, v, docs, guests, [lm])
    back = [(level, exchanged(x, "seq", mask)) for (level, mask), x in zip(visits, partial)]
    shards = (w_ff, ff_near, ff_far, exchanged(behind(ff_far, back[1][1]), "fsdp", 1))

    encoded, early_mine, early_theirs, gmerged, dd, lmf, gmid, small, gbias, *send = middle(
        levels, where, shards, o, lm, back, inputs, cotangent[0], vectors, bias_row)

    early_theirs = exchanged(early_theirs, "fsdp", 1)
    guests = [guest + (exchanged(send[level - 1], "seq", mask),) for guest, (level, mask) in zip(guests, visits)]
    nears = near_back(q, k, v, docs, gmerged, lmf, dd, 0, 8)
    early = added(early_mine, behind(early_theirs, nears[0]))
    n = FF_PART + D // 4
    up, down = chip_sum(early[:, n:]), halved(early[:, :n], rank, 0)
    gq, gk, gv = near_back(q, k, v, docs, gmerged, lmf, dd, 8, 8, nears, [early])
    far_k, far_v, *turned = far_back(k, v, docs, guests, [gq])
    back = [(level, exchanged(x, "seq", mask)) for (level, mask), x in zip(visits, turned)]
    to_near, own_part, keys_mine, keys_theirs, sums = keys_last(
        where, qkv_shards, (gk, gv, far_k, far_v), normed, [up, down])
    got = exchanged(to_near, "seq", 1)
    up, down = halved(up, rank, 1), chip_sum(down)
    keys = chip_sum(core_sum(keys_mine, keys_theirs))
    grad_tiles, late_mine, late_theirs = last(
        where, qkv_shards, gq, back, normed, inputs, gmid, vectors, small, gbias, own_part, got, sums, [up, down])
    up, down, keys = beyond(up, seq), beyond(down, seq), beyond(keys, seq)
    up, down = halved(up, rank, 0), halved(down, rank, 1)
    up, down = halved(up, rank, 2), halved(down, rank, 2)
    for bit in (1, 0, 2):
        keys = halved(keys, rank, bit)
    up, down = doubled(up, rank, 2), doubled(down, rank, 2)
    up, down = doubled(up, rank, 0), doubled(down, rank, 1)
    up, down = doubled(up, rank, 1), doubled(down, rank, 0)
    for bit in (2, 0, 1):
        keys = doubled(keys, rank, bit)
    late = direct(late_mine, late_theirs, seq).astype(f32)
    sum_up, sum_down, late_keys = [x[0].astype(f32) for x in (up, down, keys)]

    side_by_side = lambda a: a.reshape(-1, D // 4, D).swapaxes(0, 1).reshape(D // 4, -1)
    tiny = late[D // 4 : D // 4 + 16]
    mine = lax.dynamic_slice_in_dim(tiny[:8], part * cols, cols, 1)
    sum_bias = lax.dynamic_slice_in_dim(tiny[8:12], part, 1, 0).reshape(-1)
    return (
        encoded[None],
        grad_tiles[None],
        side_by_side(jnp.concatenate([late[: D // 4], late_keys], axis=0)), sum_down[FF_PART:], side_by_side(sum_up), sum_down[:FF_PART],
        mine[:2], mine[2:], sum_bias,
    )


def solution(mesh):
    tokens, rows, cols = P("fsdp", "seq", None), P("fsdp", None), P(None, "fsdp")
    return jax.shard_map(
        local,
        mesh=mesh,
        in_specs=(tokens, P("fsdp", "seq"), tokens, rows, rows, rows, rows, cols, cols, P("fsdp")),
        out_specs=(tokens, tokens, rows, rows, rows, rows, cols, cols, P("fsdp")),
        check_vma=False,
    )
```

time: 2060 us -> 396 us (0.19)
  matrix products: 481 us -> 0 us
  local copies, waits for them, and re-layouts: 497 us -> 22.6 us
  waiting for transfers between devices: 491 us -> 157 us
  blocking collectives: 322 us -> 0 us
  other arithmetic: 183 us -> 23.4 us
  Pallas kernels: 0 us -> 124 us
    dot_general x228 -> x0, matrix products: 481 us -> none  [the longest x31 91.9 us: backward_block(): jnp.einsum('hqk,hqd->hkd', grad_scores, queries, preferred_element_type=j...]
    unnamed x8 -> x0, waiting for transfers between devices: 373 us -> none
    unnamed x1 -> x0, blocking collectives: 279 us -> none
    mul x77 -> x0, local copies, waits for them, and re-layouts: 168 us -> none  [the longest x60 161 us: spread_rows(): grown_rows = tensor[:, None] * factors]
    pallas_call x0 -> x9, Pallas kernels: none -> 124 us  [the longest x1 32.9 us: middle(): kernel_call(functools.partial(middle_kernel, levels, [b[0] for b in back]...]
    reduce_sum x60 -> x1, other arithmetic: 65.9 us -> 0.06 us  [direct(): piece = jnp.sum(pieces.astype(f32), axis=0).astype(bf16)]
    another operation x30 -> x3, local copies, waits for them, and re-layouts: 49 us -> 0.27 us  [local(): stacked = jnp.stack([w[cols].reshape(-1, cols) for w in qkv_shards])]
    all_gather x4 -> x0, blocking collectives: 43.2 us -> none  [the longest x1 27.8 us: local(): all_docs = lax.all_gather(own_docs, 'seq', axis=0, tiled=True)]
  transfers between devices with their start and end apart: 54 -> 47, of which waited for: 22 -> 21; matrix products, arithmetic and copies ran while one was open for 39% -> 7% of each run, Pallas kernels for 0% -> 24%
where the time goes in v1:
time: 396 us; the launch traced here: 388 us
  waiting for transfers between devices  157 us (40%)
  Pallas kernels  124 us (31%)
  starting transfers between devices  58.8 us (15%)
  other arithmetic  23.4 us (6%)
  local copies, waits for them, and re-layouts  22.6 us (6%)
    ppermute x45, waiting for transfers between devices, exchanged(): lax.ppermute(x, axis, [(i, i ^ mask) for i in range(lax.axis_size(axis))])  150 us
    ppermute x45, starting transfers between devices, exchanged(): lax.ppermute(x, axis, [(i, i ^ mask) for i in range(lax.axis_size(axis))])  51.1 us
    pallas_call x1, Pallas kernels, middle(): kernel_call(functools.partial(middle_kernel, levels, [b[0] for b in back]...  32.9 us
    pallas_call x2, Pallas kernels, near_back(): kernel_call(functools.partial(near_back_kernel, first), after=after, grid...  26.7 us
    pallas_call x1, Pallas kernels, attend_near(): kernel_call(near_kernel, grid=(HEADS // NEAR,), in_specs=[r(T), r(2 * T),...  15 us
    convert_element_type x16, other arithmetic, added(): return (a.astype(f32) + b.astype(f32)).astype(bf16)  13.1 us
    pallas_call x1, Pallas kernels, far_back(): kernel_call(functools.partial(far_back_kernel, [v[0] for v in guests]), a...  12.9 us
    pallas_call x1, Pallas kernels, keys_last(): kernel_call(keys_kernel, after=after, in_specs=[SM] + [HB] * 4 + [VM] * 5...  12.2 us
  transfers between devices with their start and end apart: 47, of which 21 were waited for; matrix products, arithmetic and copies ran while one was open for 7% of the time, Pallas kernels for 24%

profile of v1, /device:TPU:0, one launch (start us, length us, event | category | flops | bytes accessed | tf_op | source)
XLA Modules:
  0.0 388.3 jit_solution(13392081999159438087)
XLA Ops:
  4.2 3.0 collective-permute-start.3
  7.4 1.6 collective-permute-start.4
  9.1 1.7 pad_maximum_fusion.refs_0_
  11.3 15.4 %collective-permute-done.4.x1_ref = bf16[520,768]{1,0:T(8,128)(2,1)S(1)} collective-permute-done((bf16[520,768]{1,0:T(8,128)(2,1)S(1)}, bf16[520,768]{1,0:T(8,128)(2,1)S(1)}, u32[]{:S(2)}, u32[]{:S(2)}) %collective-permute-start.4) | collective-permute-done | bytes 798752 | tf_op jit(solution)/shard_map/ppermute | solution.py:726
  26.7 1.8 collective-permute-done.3.w2.refs_5_
  29.6 1.5 collective-permute-done.5.w3.refs_6_
  33.6 8.5 %project.1 = (bf16[768,512]{1,0:T(8,128)(2,1)}, bf16[768,1024]{1,0:T(8,128)(2,1)}, bf16[768,1024]{1,0:T(8,128)(2,1)}, bf16[1024,768]{1,0:T(8,128)(2,1)}, bf16[51...) custom-call(s32[4]{0:T(128)} %pad_add_fusion.where_ref.refs_2_, ...), custom_call_target="tpu_custom_call" | custom-call | flops 1000000000 | bytes 1000 | tf_op jit(solution)/shard_map/project/pallas_call | solution.py:465
  42.1 2.2 collective-permute-start.6
  44.4 2.6 collective-permute-start.7
  47.0 15.0 %near.1 = (f32[768,512]{1,0:T(8,128)}, f32[16,1,512]{2,1,0:T(1,128)}) custom-call(bf16[768,512]{1,0:T(8,128)(2,1)} %get-tuple-element.56.q_ref.refs_1_, bf16[768,1024]{1,0:T(8,128)(2,1)} %get-tuple-element.57.k_ref.refs_1_.refs_2_, bf16[768,1024]{1,0:T(8,128)(2,1)} %get-tuple-element.58.v_ref.refs_2_.refs_3_, ...), custom_call_target="tpu_custom_call" | custom-call | flops 1000000000 | bytes 1000 | tf_op jit(solution)/shard_map/near/pallas_call | solution.py:310
  62.0 3.1 collective-permute-done.8.refs_8_.refs_9_.refs_10_.refs_11_
  65.9 7.1 %far.1 = (bf16[1024,256]{1,0:T(8,128)(2,1)}, bf16[1024,128]{1,0:T(8,128)(2,1)}, bf16[1024,128]{1,0:T(8,128)(2,1)}) custom-call(f32[16,1,512]{2,1,0:T(1,128)} %get-tuple-element.60.refs_0_.refs_5_, bf16[768,1024]{1,0:T(8,128)(2,1)} %get-tuple-element.57.k_ref.refs_1_.refs_2_, bf16[768,1024]{1,0:T(8,128)(2,1)} %get-tuple-element.58.v_ref.refs_2_.refs_3_, ...), custom_call_target="tpu_custom_call" | custom-call | flops 1000000000 | bytes 1000 | tf_op jit(solution)/shard_map/far/pallas_call | solution.py:331
  73.0 1.8 collective-permute-start.9
  74.8 11.3 %collective-permute-done.9.refs_11_ = bf16[1024,128]{1,0:T(8,128)(2,1)S(1)} collective-permute-done((bf16[1024,128]{1,0:T(8,128)(2,1)}, bf16[1024,128]{1,0:T(8,128)(2,1)S(1)}, u32[]{:S(2)}, u32[]{:S(2)}) %collective-permute-start.9) | collective-permute-done | bytes 262176 | tf_op jit(solution)/shard_map/ppermute | solution.py:726
  86.5 2.5 collective-permute-start.12
  89.7 17.5 %collective-permute-done.12.refs_12_ = bf16[1024,128]{1,0:T(8,128)(2,1)} collective-permute-done((bf16[1024,128]{1,0:T(8,128)(2,1)}, bf16[1024,128]{1,0:T(8,128)(2,1)}, u32[]{:S(2)}, u32[]{:S(2)}) %collective-permute-start.12) | collective-permute-done | bytes 262176 | tf_op jit(solution)/shard_map/ppermute | solution.py:726
  107.3 1.5 copy-done.15
  108.9 32.9 %middle.1 = (bf16[512,768]{1,0:T(8,128)(2,1)}, bf16[2,1728,768]{2,1,0:T(8,128)(2,1)}, bf16[2,1728,768]{2,1,0:T(8,128)(2,1)}, bf16[768,512]{1,0:T(8,128)(2,1)}, f...) custom-call(s32[4]{0:T(128)} %pad_add_fusion.where_ref.refs_2_, ...), custom_call_target="tpu_custom_call" | custom-call | flops 1000000000 | bytes 1000 | tf_op jit(solution)/shard_map/middle/pallas_call | solution.py:614
  141.9 13.4 %near_back.2 = (bf16[768,512]{1,0:T(8,128)(2,1)}, bf16[768,1024]{1,0:T(8,128)(2,1)}, bf16[768,1024]{1,0:T(8,128)(2,1)}) custom-call(bf16[768,512]{1,0:T(8,128)(2,1)} %get-tuple-element.56.q_ref.refs_1_, bf16[768,1024]{1,0:T(8,128)(2,1)} %get-tuple-element.57.k_ref.refs_1_.refs_2_, bf16[768,1024]{1,0:T(8,128)(2,1)} %get-tuple-element.58.v_ref.refs_2_.refs_3_, ...), custom_call_target="tpu_custom_call" | custom-call | flops 1000000000 | bytes 1000 | tf_op jit(solution)/shard_map/near_back/pallas_call | solution.py:346
  155.3 3.8 add_convert_fusion.refs_0_
  159.0 2.3 copy-done
  161.5 1.6 collective-permute-start.14
  163.0 2.0 slice.115
  165.1 1.6 copy-done.4
  166.8 1.6 collective-permute-start.16
  168.4 21.6 %collective-permute-done.14 = bf16[1,768,768]{2,1,0:T(8,128)(2,1)} collective-permute-done((bf16[1,768,768]{2,1,0:T(8,128)(2,1)S(1)}, bf16[1,768,768]{2,1,0:T(8,128)(2,1)}, u32[]{:S(2)}, u32[]{:S(2)}) %collective-permute-start.14) | collective-permute-done | bytes 1179680 | tf_op jit(solution)/shard_map/ppermute | solution.py:726
  190.0 1.9 add_convert_fusion.3.refs_0_
  192.0 2.0 collective-permute-start.19
  194.0 2.4 collective-permute-start.20
  196.4 13.4 %near_back.3 = (bf16[768,512]{1,0:T(8,128)(2,1)}, bf16[768,1024]{1,0:T(8,128)(2,1)}, bf16[768,1024]{1,0:T(8,128)(2,1)}) custom-call(bf16[2,1728,768]{2,1,0:T(8,128)(2,1)} %copy-done, bf16[768,512]{1,0:T(8,128)(2,1)} %get-tuple-element.56.q_ref.refs_1_, ...), custom_call_target="tpu_custom_call", output_to_operand_aliasing={{0}: (8, {}), {1}: (9, {}), {2}: (10, {})} | custom-call | flops 1000000000 | bytes 1000 | tf_op jit(solution)/shard_map/near_back/pallas_call | solution.py:346
  209.8 1.7 collective-permute-done.19.refs_9_
  211.5 6.7 %collective-permute-done.20.refs_12_ = bf16[1024,128]{1,0:T(8,128)(2,1)} collective-permute-done((bf16[1024,128]{1,0:T(8,128)(2,1)}, bf16[1024,128]{1,0:T(8,128)(2,1)}, u32[]{:S(2)}, u32[]{:S(2)}) %collective-permute-start.20) | collective-permute-done | bytes 262176 | tf_op jit(solution)/shard_map/ppermute | solution.py:726
  218.2 12.9 %far_back.1 = (bf16[768,1024]{1,0:T(8,128)(2,1)}, bf16[768,1024]{1,0:T(8,128)(2,1)}, bf16[768,256]{1,0:T(8,128)(2,1)}, bf16[768,128]{1,0:T(8,128)(2,1)}, bf16[768,128]{1,0:T(8,128)(2,1)}) custom-call(bf16[768,512]{1,0:T(8,128)(2,1)} %get-tuple-element.79.refs_0_.refs_7_, bf16[768,1024]{1,0:T(8,128)(2,1)} %get-tuple-element.57.k_ref.refs_1_.refs_2_, ...), custom_call_target="tpu_custom_call" | custom-call | flops 1000000000 | bytes 1000 | tf_op jit(solution)/shard_map/far_back/pallas_call | solution.py:369
  232.4 1.6 collective-permute-start.40
  234.0 1.7 add_convert_fusion.1.refs_1_
  236.8 1.5 collective-permute-start.17
  238.3 12.2 %keys_last.1 = (bf16[512,768]{1,0:T(8,128)(2,1)}, f32[512,768]{1,0:T(8,128)}, bf16[2,384,768]{2,1,0:T(8,128)(2,1)}, bf16[2,384,768]{2,1,0:T(8,128)(2,1)}, f32[8,768]{1,0:T(8,128)}) custom-call(bf16[1,768,768]{2,1,0:T(8,128)(2,1)} %copy-done.6, bf16[2,480,768]{2,1,0:T(8,128)(2,1)} %copy-done.2, s32[4]{0:T(128)} %pad_add_fusion.where_ref.refs_2_, ...), custom_call_target="tpu_custom_call" | custom-call | flops 1000000000 | bytes 1000 | tf_op jit(solution)/shard_map/keys_last/pallas_call | solution.py:665
  251.3 2.7 collective-permute-start.21
  254.2 6.0 %collective-permute-done.41 = bf16[1,96,768]{2,1,0:T(8,128)(2,1)S(1)} collective-permute-done((bf16[1,96,768]{2,1,0:T(8,128)(2,1)S(1)}, bf16[1,96,768]{2,1,0:T(8,128)(2,1)S(1)}, u32[]{:S(2)}, u32[]{:S(2)}) %collective-permute-start.41) | collective-permute-done | bytes 147488 | tf_op jit(solution)/shard_map/ppermute | solution.py:726
  260.2 1.9 collective-permute-start.23
  262.3 1.4 add_convert_fusion.5.refs_1_
  263.7 4.6 %collective-permute-done.22.refs_9_ = bf16[768,128]{1,0:T(8,128)(2,1)S(1)} collective-permute-done((bf16[768,128]{1,0:T(8,128)(2,1)}, bf16[768,128]{1,0:T(8,128)(2,1)S(1)}, u32[]{:S(2)}, u32[]{:S(2)}) %collective-permute-start.22) | collective-permute-done | bytes 196640 | tf_op jit(solution)/shard_map/ppermute | solution.py:726
  268.3 6.1 %collective-permute-done.23.refs_10_ = bf16[768,128]{1,0:T(8,128)(2,1)S(1)} collective-permute-done((bf16[768,128]{1,0:T(8,128)(2,1)S(1)}, bf16[768,128]{1,0:T(8,128)(2,1)S(1)}, u32[]{:S(2)}, u32[]{:S(2)}) %collective-permute-start.23) | collective-permute-done | bytes 196640 | tf_op jit(solution)/shard_map/ppermute | solution.py:726
  274.4 6.3 %collective-permute-start.35 = (bf16[1,240,768]{2,1,0:T(8,128)(2,1)S(1)}, bf16[1,240,768]{2,1,0:T(8,128)(2,1)S(1)}, u32[]{:S(2)}, u32[]{:S(2)}) collective-permute-start(bf16[1,240,768]{2,1,0:T(8,128)(2,1)S(1)} %constant_dynamic-slice_fusion.5), channel_id=1, source_target_pairs={{0,2},{1,3},{2,0},{3,1},{4,6},{5,7},{6,4},{7,5},{8,10},{9,11},{10,... | collective-permute-start | bytes 1105928 | tf_op jit(solution)/shard_map/ppermute | solution.py:726
  281.7 8.9 %last.1 = (bf16[512,768]{1,0:T(8,128)(2,1)}, bf16[2,256,768]{2,1,0:T(8,128)(2,1)}, bf16[2,256,768]{2,1,0:T(8,128)(2,1)}) custom-call(bf16[1,384,768]{2,1,0:T(8,128)(2,1)} %copy-done.11, bf16[1,480,768]{2,1,0:T(8,128)(2,1)} %copy-done.9, s32[4]{0:T(128)} %pad_add_fusion.where_ref.refs_2_, bf16[200,2304]{1,0:T(8,128)(2,1)} %copy-done.1, ...), custom_call_target="tpu_custom_call" | custom-call | flops 1000000000 | bytes 1000 | tf_op jit(solution)/shard_map/last/pallas_call | solution.py:713
  290.8 1.6 collective-permute-start.43
  294.0 6.2 %collective-permute-done.43 = bf16[1,192,768]{2,1,0:T(8,128)(2,1)S(1)} collective-permute-done((bf16[1,192,768]{2,1,0:T(8,128)(2,1)S(1)}, bf16[1,192,768]{2,1,0:T(8,128)(2,1)S(1)}, u32[]{:S(2)}, u32[]{:S(2)}) %collective-permute-start.43) | collective-permute-done | bytes 294944 | tf_op jit(solution)/shard_map/ppermute | solution.py:726
  300.5 4.3 %collective-permute-done.36 = bf16[1,120,768]{2,1,0:T(8,128)(2,1)S(1)} collective-permute-done((bf16[1,120,768]{2,1,0:T(8,128)(2,1)S(1)}, bf16[1,120,768]{2,1,0:T(8,128)(2,1)S(1)}, u32[]{:S(2)}, u32[]{:S(2)}) %collective-permute-start.36) | collective-permute-done | bytes 184352 | tf_op jit(solution)/shard_map/ppermute | solution.py:726
  305.8 11.3 %collective-permute-done.37 = bf16[1,120,768]{2,1,0:T(8,128)(2,1)S(1)} collective-permute-done((bf16[1,120,768]{2,1,0:T(8,128)(2,1)S(1)}, bf16[1,120,768]{2,1,0:T(8,128)(2,1)S(1)}, u32[]{:S(2)}, u32[]{:S(2)}) %collective-permute-start.37) | collective-permute-done | bytes 184352 | tf_op jit(solution)/shard_map/ppermute | solution.py:726
  317.2 3.0 collective-permute-start.38
  321.5 1.6 collective-permute-start.29
  323.4 12.1 %collective-permute-done.29 = bf16[1,192,768]{2,1,0:T(8,128)(2,1)S(1)} collective-permute-done((bf16[1,192,768]{2,1,0:T(8,128)(2,1)S(1)}, bf16[1,192,768]{2,1,0:T(8,128)(2,1)S(1)}, u32[]{:S(2)}, u32[]{:S(2)}) %collective-permute-start.29) | collective-permute-done | bytes 294944 | tf_op jit(solution)/shard_map/ppermute | solution.py:726
  336.3 4.7 %collective-permute-done.30 = bf16[1,96,768]{2,1,0:T(8,128)(2,1)S(1)} collective-permute-done((bf16[1,96,768]{2,1,0:T(8,128)(2,1)S(1)}, bf16[1,96,768]{2,1,0:T(8,128)(2,1)S(1)}, u32[]{:S(2)}, u32[]{:S(2)}) %collective-permute-start.30) | collective-permute-done | bytes 147488 | tf_op jit(solution)/shard_map/ppermute | solution.py:726
  342.9 1.5 collective-permute-start.39
  344.4 3.4 collective-permute-done.31
  348.8 4.2 %all-to-all-start = ((bf16[8,32,768]{2,1,0:T(8,128)(2,1)}), bf16[8,32,768]{2,1,0:T(8,128)(2,1)S(1)}, u32[]{:S(2)}, u32[]{:S(2)}) async-start(bf16[8,32,768]{2,1,0:T(8,128)(2,1)} %bitcast.15), calls=%async_computation | async-start | bytes 786432 | tf_op jit(solution)/shard_map/all_to_all | solution.py:768
  353.0 1.5 collective-permute-done.32
  355.3 1.7 copy.33
  357.0 9.7 %collective-permute-done.33 = bf16[1,96,768]{2,1,0:T(8,128)(2,1)S(1)} collective-permute-done((bf16[1,96,768]{2,1,0:T(8,128)(2,1)S(1)}, bf16[1,96,768]{2,1,0:T(8,128)(2,1)S(1)}, u32[]{:S(2)}, u32[]{:S(2)}) %collective-permute-start.33) | collective-permute-done | bytes 147488 | tf_op jit(solution)/shard_map/ppermute | solution.py:726
  366.7 2.0 collective-permute-start.34
  369.6 3.5 all-to-all-start.1
  374.2 1.6 convert_bitcast_fusion.1
  376.0 7.0 %all-to-all-done.1 = bf16[8,32,768]{2,1,0:T(8,128)(2,1)S(1)} async-done(((bf16[8,32,768]{2,1,0:T(8,128)(2,1)}), bf16[8,32,768]{2,1,0:T(8,128)(2,1)S(1)}, u32[]{:S(2)}, u32[]{:S(2)}) %all-to-all-start.1) | async-done | bytes 393248 | tf_op jit(solution)/shard_map/all_to_all | solution.py:770
  384.4 1.5 copy.34
  (196 shorter events, 29.6 us)
Async XLA Ops:
  0.6 6.6 %copy-start.30 = (s32[1,512]{1,0:T(1,128)S(1)}, s32[1,512]{1,0:T(1,128)}, u32[]{:S(2)}) copy-start(s32[1,512]{1,0:T(1,128)} %docs_ref.1) | copy-start | bytes 6148
  0.7 6.6 %copy-start.14 = (bf16[1,512,768]{2,1,0:T(8,128)(2,1)S(1)}, bf16[1,512,768]{2,1,0:T(8,128)(2,1)}, u32[]{:S(2)}) copy-start(bf16[1,512,768]{2,1,0:T(8,128)(2,1)} %param.10) | copy-start | bytes 2359300
  4.2 7.1 %copy-start.1 = (bf16[200,2304]{1,0:T(8,128)(2,1)}, bf16[200,2304]{1,0:T(8,128)(2,1)S(1)}, u32[]{:S(2)}) copy-start(bf16[200,2304]{1,0:T(8,128)(2,1)S(1)} %fusion.2.w0.refs_3_) | copy-start | bytes 2764804
  4.2 24.3 %collective-permute-start.3 = (bf16[200,2304]{1,0:T(8,128)(2,1)S(1)}, bf16[200,2304]{1,0:T(8,128)(2,1)S(1)}, u32[]{:S(2)}, u32[]{:S(2)}) collective-permute-start(bf16[200,2304]{1,0:T(8,128)(2,1)S(1)} %fusion.2.w0.refs_3_), channel_id=1, source_target_pairs={{0,16},{8,24},{16,0},{24,8},{1,17},{9,25},{17,1},{25,9},{2,18},{10... | collective-permute-start | bytes 2764808 | tf_op jit(solution)/shard_map/ppermute | solution.py:726
  7.4 19.3 %collective-permute-start.4 = (bf16[520,768]{1,0:T(8,128)(2,1)S(1)}, bf16[520,768]{1,0:T(8,128)(2,1)S(1)}, u32[]{:S(2)}, u32[]{:S(2)}) collective-permute-start(bf16[520,768]{1,0:T(8,128)(2,1)S(1)} %fusion.3), channel_id=1, source_target_pairs={{0,1},{1,0},{2,3},{3,2},{4,5},{5,4},{6,7},{7,6},{8,9},{9,8},{10,11... | collective-permute-start | bytes 2396168 | tf_op jit(solution)/shard_map/ppermute | solution.py:726
  9.0 23.0 %copy-start.29 = (bf16[1,12,192]{2,1,0:T(8,128)(2,1)S(1)}, bf16[1,12,192]{2,1,0:T(8,128)(2,1)}, u32[]{:S(2)}) copy-start(bf16[1,12,192]{2,1,0:T(8,128)(2,1)} %get-tuple-element.125) | copy-start | bytes 13828
  10.8 75.3 %collective-permute-start.1 = (bf16[1728,768]{1,0:T(8,128)(2,1)}, bf16[1728,768]{1,0:T(8,128)(2,1)}, u32[]{:S(2)}, u32[]{:S(2)}) collective-permute-start(bf16[1728,768]{1,0:T(8,128)(2,1)} %pad_maximum_fusion.refs_0_), channel_id=1, source_target_pairs={{0,16},{8,24},{16,0},{24,8},{1,17},{9,25},{17,1},{25,9},{2,18},{10... | collective-permute-start | bytes 7962632 | tf_op jit(solution)/shard_map/ppermute | solution.py:726
  11.3 18.2 %collective-permute-start.2 = (bf16[200,2304]{1,0:T(8,128)(2,1)S(1)}, bf16[200,2304]{1,0:T(8,128)(2,1)S(1)}, u32[]{:S(2)}, u32[]{:S(2)}) collective-permute-start(bf16[200,2304]{1,0:T(8,128)(2,1)S(1)} %fusion.2.w0.refs_3_), channel_id=1, source_target_pairs={{0,8},{8,0},{16,24},{24,16},{1,9},{9,1},{17,25},{25,17},{2,10},{10... | collective-permute-start | bytes 2764808 | tf_op jit(solution)/shard_map/ppermute | solution.py:726
  28.5 2.6 collective-permute-start.5
  42.1 22.9 %collective-permute-start.6 = (bf16[784,256]{1,0:T(8,128)(2,1)}, bf16[784,256]{1,0:T(8,128)(2,1)S(1)}, u32[]{:S(2)}, u32[]{:S(2)}) collective-permute-start(bf16[784,256]{1,0:T(8,128)(2,1)} %get-tuple-element.61), channel_id=1, source_target_pairs={{0,2},{1,3},{2,0},{3,1},{4,6},{5,7},{6,4},{7,5},{8,10},{9,11},{10,... | collective-permute-start | bytes 1204232 | tf_op jit(solution)/shard_map/ppermute | solution.py:726
  44.4 17.6 %collective-permute-start.7 = (bf16[784,128]{1,0:T(8,128)(2,1)}, bf16[784,128]{1,0:T(8,128)(2,1)S(1)}, u32[]{:S(2)}, u32[]{:S(2)}) collective-permute-start(bf16[784,128]{1,0:T(8,128)(2,1)} %get-tuple-element.62), channel_id=1, source_target_pairs={{0,4},{1,5},{2,6},{3,7},{4,0},{5,1},{6,2},{7,3},{8,12},{9,13},{10,... | collective-permute-start | bytes 602120 | tf_op jit(solution)/shard_map/ppermute | solution.py:726
  46.9 18.1 %collective-permute-start.8 = (bf16[784,128]{1,0:T(8,128)(2,1)}, bf16[784,128]{1,0:T(8,128)(2,1)S(1)}, u32[]{:S(2)}, u32[]{:S(2)}) collective-permute-start(bf16[784,128]{1,0:T(8,128)(2,1)} %get-tuple-element.62), channel_id=1, source_target_pairs={{0,6},{1,7},{2,4},{3,5},{4,2},{5,3},{6,0},{7,1},{8,14},{9,15},{10,... | collective-permute-start | bytes 602120 | tf_op jit(solution)/shard_map/ppermute | solution.py:726
  73.0 13.0 %collective-permute-start.9 = (bf16[1024,128]{1,0:T(8,128)(2,1)}, bf16[1024,128]{1,0:T(8,128)(2,1)S(1)}, u32[]{:S(2)}, u32[]{:S(2)}) collective-permute-start(bf16[1024,128]{1,0:T(8,128)(2,1)} %get-tuple-element.63), channel_id=1, source_target_pairs={{0,4},{1,5},{2,6},{3,7},{4,0},{5,1},{6,2},{7,3},{8,12},{9,13},{10,... | collective-permute-start | bytes 786440 | tf_op jit(solution)/shard_map/ppermute | solution.py:726
  74.8 32.5 %collective-permute-start = (bf16[1728,768]{1,0:T(8,128)(2,1)}, bf16[1728,768]{1,0:T(8,128)(2,1)S(1)}, u32[]{:S(2)}, u32[]{:S(2)}) collective-permute-start(bf16[1728,768]{1,0:T(8,128)(2,1)} %pad_maximum_fusion.refs_0_), channel_id=1, source_target_pairs={{0,8},{8,0},{16,24},{24,16},{1,9},{9,1},{17,25},{25,17},{2,10},{10... | collective-permute-start | bytes 7962632 | tf_op jit(solution)/shard_map/ppermute | solution.py:726
  86.0 21.2 %copy-start.25 = (bf16[1024,128]{1,0:T(8,128)(2,1)}, bf16[1024,128]{1,0:T(8,128)(2,1)S(1)}, u32[]{:S(2)}) copy-start(bf16[1024,128]{1,0:T(8,128)(2,1)S(1)} %collective-permute-done.9.refs_11_) | copy-start | bytes 786436
  86.0 21.2 %collective-permute-start.10 = (bf16[1728,768]{1,0:T(8,128)(2,1)}, bf16[1728,768]{1,0:T(8,128)(2,1)}, u32[]{:S(2)}, u32[]{:S(2)}) collective-permute-start(bf16[1728,768]{1,0:T(8,128)(2,1)} %collective-permute-done.1.refs_2_), channel_id=1, source_target_pairs={{0,8},{8,0},{16,24},{24,16},{1,9},{9,1},{17,25},{25,17},{2,10},{10... | collective-permute-start | bytes 7962632 | tf_op jit(solution)/shard_map/ppermute | solution.py:726
  86.0 21.2 %collective-permute-start.11 = (bf16[1024,256]{1,0:T(8,128)(2,1)}, bf16[1024,256]{1,0:T(8,128)(2,1)S(1)}, u32[]{:S(2)}, u32[]{:S(2)}) collective-permute-start(bf16[1024,256]{1,0:T(8,128)(2,1)} %get-tuple-element.67), channel_id=1, source_target_pairs={{0,2},{1,3},{2,0},{3,1},{4,6},{5,7},{6,4},{7,5},{8,10},{9,11},{10,... | collective-permute-start | bytes 1572872 | tf_op jit(solution)/shard_map/ppermute | solution.py:726
  86.5 20.7 %collective-permute-start.12 = (bf16[1024,128]{1,0:T(8,128)(2,1)}, bf16[1024,128]{1,0:T(8,128)(2,1)}, u32[]{:S(2)}, u32[]{:S(2)}) collective-permute-start(bf16[1024,128]{1,0:T(8,128)(2,1)} %get-tuple-element.68), channel_id=1, source_target_pairs={{0,6},{1,7},{2,4},{3,5},{4,2},{5,3},{6,0},{7,1},{8,14},{9,15},{10,... | collective-permute-start | bytes 786440 | tf_op jit(solution)/shard_map/ppermute | solution.py:726
  141.8 13.4 %collective-permute-start.13 = (bf16[2,1728,768]{2,1,0:T(8,128)(2,1)}, bf16[2,1728,768]{2,1,0:T(8,128)(2,1)S(1)}, u32[]{:S(2)}, u32[]{:S(2)}) collective-permute-start(bf16[2,1728,768]{2,1,0:T(8,128)(2,1)} %get-tuple-element.71), channel_id=1, source_target_pairs={{0,8},{8,0},{16,24},{24,16},{1,9},{9,1},{17,25},{25,17},{2,10},{10... | collective-permute-start | bytes 15925256 | tf_op jit(solution)/shard_map/ppermute | solution.py:726
  161.5 28.5 %collective-permute-start.14 = (bf16[1,768,768]{2,1,0:T(8,128)(2,1)S(1)}, bf16[1,768,768]{2,1,0:T(8,128)(2,1)}, u32[]{:S(2)}, u32[]{:S(2)}) collective-permute-start(bf16[1,768,768]{2,1,0:T(8,128)(2,1)S(1)} %slice.114), channel_id=1, source_target_pairs={{0,16},{8,24},{16,0},{24,8},{1,17},{9,25},{17,1},{25,9},{2,18},{10... | collective-permute-start | bytes 3538952 | tf_op jit(solution)/shard_map/ppermute | solution.py:726
  166.8 67.2 %collective-permute-start.16 = (bf16[2,480,768]{2,1,0:T(8,128)(2,1)S(1)}, bf16[2,480,768]{2,1,0:T(8,128)(2,1)}, u32[]{:S(2)}, u32[]{:S(2)}) collective-permute-start(bf16[2,480,768]{2,1,0:T(8,128)(2,1)S(1)} %constant_dynamic-slice_fusion.9), channel_id=1, source_target_pairs={{0,1},{1,0},{2,3},{3,2},{4,5},{5,4},{6,7},{7,6},{8,9},{9,8},{10,11... | collective-permute-start | bytes 4423688 | tf_op jit(solution)/shard_map/ppermute | solution.py:726
  168.4 49.8 %collective-permute-start.18 = (bf16[1024,256]{1,0:T(8,128)(2,1)}, bf16[1024,256]{1,0:T(8,128)(2,1)}, u32[]{:S(2)}, u32[]{:S(2)}) collective-permute-start(bf16[1024,256]{1,0:T(8,128)(2,1)} %get-tuple-element.80), channel_id=1, source_target_pairs={{0,2},{1,3},{2,0},{3,1},{4,6},{5,7},{6,4},{7,5},{8,10},{9,11},{10,... | collective-permute-start | bytes 1572872 | tf_op jit(solution)/shard_map/ppermute | solution.py:726
  191.9 39.2 %copy-start.6 = (bf16[1,768,768]{2,1,0:T(8,128)(2,1)}, bf16[1,768,768]{2,1,0:T(8,128)(2,1)S(1)}, u32[]{:S(2)}) copy-start(bf16[1,768,768]{2,1,0:T(8,128)(2,1)S(1)} %add_convert_fusion.3.refs_0_) | copy-start | bytes 3538948
  192.0 39.2 %collective-permute-start.15 = (bf16[1,384,768]{2,1,0:T(8,128)(2,1)S(1)}, bf16[1,384,768]{2,1,0:T(8,128)(2,1)}, u32[]{:S(2)}, u32[]{:S(2)}) collective-permute-start(bf16[1,384,768]{2,1,0:T(8,128)(2,1)S(1)} %constant_dynamic-slice_fusion.10), channel_id=1, source_target_pairs={{0,2},{1,3},{2,0},{3,1},{4,6},{5,7},{6,4},{7,5},{8,10},{9,11},{10,... | collective-permute-start | bytes 1769480 | tf_op jit(solution)/shard_map/ppermute | solution.py:726
  192.0 19.4 %collective-permute-start.19 = (bf16[1024,128]{1,0:T(8,128)(2,1)}, bf16[1024,128]{1,0:T(8,128)(2,1)S(1)}, u32[]{:S(2)}, u32[]{:S(2)}) collective-permute-start(bf16[1024,128]{1,0:T(8,128)(2,1)} %get-tuple-element.81), channel_id=1, source_target_pairs={{0,4},{1,5},{2,6},{3,7},{4,0},{5,1},{6,2},{7,3},{8,12},{9,13},{10,... | collective-permute-start | bytes 786440 | tf_op jit(solution)/shard_map/ppermute | solution.py:726
  194.0 24.2 %collective-permute-start.20 = (bf16[1024,128]{1,0:T(8,128)(2,1)}, bf16[1024,128]{1,0:T(8,128)(2,1)}, u32[]{:S(2)}, u32[]{:S(2)}) collective-permute-start(bf16[1024,128]{1,0:T(8,128)(2,1)} %get-tuple-element.81), channel_id=1, source_target_pairs={{0,6},{1,7},{2,4},{3,5},{4,2},{5,3},{6,0},{7,1},{8,14},{9,15},{10,... | collective-permute-start | bytes 786440 | tf_op jit(solution)/shard_map/ppermute | solution.py:726
  211.5 6.7 %copy-start.26 = (bf16[1024,128]{1,0:T(8,128)(2,1)}, bf16[1024,128]{1,0:T(8,128)(2,1)S(1)}, u32[]{:S(2)}) copy-start(bf16[1024,128]{1,0:T(8,128)(2,1)S(1)} %collective-permute-done.19.refs_9_) | copy-start | bytes 786436
  218.2 15.8 %copy-start.5 = (bf16[2,960,768]{2,1,0:T(8,128)(2,1)S(1)}, bf16[2,960,768]{2,1,0:T(8,128)(2,1)}, u32[]{:S(2)}) copy-start(bf16[2,960,768]{2,1,0:T(8,128)(2,1)} %copy-done.4) | copy-start | bytes 8847364
  232.3 18.7 %copy-start.11 = (bf16[1,384,768]{2,1,0:T(8,128)(2,1)}, bf16[1,384,768]{2,1,0:T(8,128)(2,1)S(1)}, u32[]{:S(2)}) copy-start(bf16[1,384,768]{2,1,0:T(8,128)(2,1)S(1)} %add_convert_fusion.7.refs_0_) | copy-start | bytes 1769476
  232.4 18.7 %collective-permute-start.40 = (bf16[1,192,768]{2,1,0:T(8,128)(2,1)S(1)}, bf16[1,192,768]{2,1,0:T(8,128)(2,1)S(1)}, u32[]{:S(2)}, u32[]{:S(2)}) collective-permute-start(bf16[1,192,768]{2,1,0:T(8,128)(2,1)S(1)} %constant_dynamic-slice_fusion.3), channel_id=1, source_target_pairs={{0,1},{1,0},{2,3},{3,2},{4,5},{5,4},{6,7},{7,6},{8,9},{9,8},{10,11... | collective-permute-start | bytes 884744 | tf_op jit(solution)/shard_map/ppermute | solution.py:726
  236.8 25.4 %collective-permute-start.17 = (bf16[1,480,768]{2,1,0:T(8,128)(2,1)}, bf16[1,480,768]{2,1,0:T(8,128)(2,1)}, u32[]{:S(2)}, u32[]{:S(2)}) collective-permute-start(bf16[1,480,768]{2,1,0:T(8,128)(2,1)} %slice.117), channel_id=1, source_target_pairs={{0,16},{8,24},{16,0},{24,8},{1,17},{9,25},{17,1},{25,9},{2,18},{10... | collective-permute-start | bytes 2211848 | tf_op jit(solution)/shard_map/ppermute | solution.py:726
  238.3 21.9 %copy-start.32 = (bf16[768,128]{1,0:T(8,128)(2,1)S(1)}, bf16[768,128]{1,0:T(8,128)(2,1)}, u32[]{:S(2)}) copy-start(bf16[768,128]{1,0:T(8,128)(2,1)} %get-tuple-element.84) | copy-start | bytes 589828
  250.5 11.8 %copy-start.3 = (bf16[2,480,768]{2,1,0:T(8,128)(2,1)S(1)}, bf16[2,480,768]{2,1,0:T(8,128)(2,1)}, u32[]{:S(2)}) copy-start(bf16[2,480,768]{2,1,0:T(8,128)(2,1)} %copy-done.2) | copy-start | bytes 4423684
  250.5 30.2 %collective-permute-start.24 = (bf16[512,768]{1,0:T(8,128)(2,1)}, bf16[512,768]{1,0:T(8,128)(2,1)S(1)}, u32[]{:S(2)}, u32[]{:S(2)}) collective-permute-start(bf16[512,768]{1,0:T(8,128)(2,1)} %get-tuple-element.94), channel_id=1, source_target_pairs={{0,1},{1,0},{2,3},{3,2},{4,5},{5,4},{6,7},{7,6},{8,9},{9,8},{10,11... | collective-permute-start | bytes 2359304 | tf_op jit(solution)/shard_map/ppermute | solution.py:726
  251.2 9.0 %collective-permute-start.41 = (bf16[1,96,768]{2,1,0:T(8,128)(2,1)S(1)}, bf16[1,96,768]{2,1,0:T(8,128)(2,1)S(1)}, u32[]{:S(2)}, u32[]{:S(2)}) collective-permute-start(bf16[1,96,768]{2,1,0:T(8,128)(2,1)S(1)} %constant_dynamic-slice_fusion.2), channel_id=1, source_target_pairs={{0,4},{1,5},{2,6},{3,7},{4,0},{5,1},{6,2},{7,3},{8,12},{9,13},{10,... | collective-permute-start | bytes 442376 | tf_op jit(solution)/shard_map/ppermute | solution.py:726
  251.3 29.4 %collective-permute-start.21 = (bf16[768,256]{1,0:T(8,128)(2,1)}, bf16[768,256]{1,0:T(8,128)(2,1)S(1)}, u32[]{:S(2)}, u32[]{:S(2)}) collective-permute-start(bf16[768,256]{1,0:T(8,128)(2,1)} %get-tuple-element.82), channel_id=1, source_target_pairs={{0,2},{1,3},{2,0},{3,1},{4,6},{5,7},{6,4},{7,5},{8,10},{9,11},{10,... | collective-permute-start | bytes 1179656 | tf_op jit(solution)/shard_map/ppermute | solution.py:726
  254.0 14.3 %collective-permute-start.22 = (bf16[768,128]{1,0:T(8,128)(2,1)}, bf16[768,128]{1,0:T(8,128)(2,1)S(1)}, u32[]{:S(2)}, u32[]{:S(2)}) collective-permute-start(bf16[768,128]{1,0:T(8,128)(2,1)} %get-tuple-element.83), channel_id=1, source_target_pairs={{0,4},{1,5},{2,6},{3,7},{4,0},{5,1},{6,2},{7,3},{8,12},{9,13},{10,... | collective-permute-start | bytes 589832 | tf_op jit(solution)/shard_map/ppermute | solution.py:726
  260.2 14.2 %collective-permute-start.23 = (bf16[768,128]{1,0:T(8,128)(2,1)S(1)}, bf16[768,128]{1,0:T(8,128)(2,1)S(1)}, u32[]{:S(2)}, u32[]{:S(2)}) collective-permute-start(bf16[768,128]{1,0:T(8,128)(2,1)S(1)} %copy-done.32), channel_id=1, source_target_pairs={{0,6},{1,7},{2,4},{3,5},{4,2},{5,3},{6,0},{7,1},{8,14},{9,15},{10,... | collective-permute-start | bytes 589832 | tf_op jit(solution)/shard_map/ppermute | solution.py:726
  262.2 6.1 %copy-start.31 = (bf16[2,384,768]{2,1,0:T(8,128)(2,1)S(1)}, bf16[2,384,768]{2,1,0:T(8,128)(2,1)}, u32[]{:S(2)}) copy-start(bf16[2,384,768]{2,1,0:T(8,128)(2,1)} %get-tuple-element.100) | copy-start | bytes 3538948
  262.2 28.5 %collective-permute-start.42 = (bf16[1,96,768]{2,1,0:T(8,128)(2,1)S(1)}, bf16[1,96,768]{2,1,0:T(8,128)(2,1)S(1)}, u32[]{:S(2)}, u32[]{:S(2)}) collective-permute-start(bf16[1,96,768]{2,1,0:T(8,128)(2,1)S(1)} %add_convert_fusion.12), channel_id=1, source_target_pairs={{0,4},{1,5},{2,6},{3,7},{4,0},{5,1},{6,2},{7,3},{8,12},{9,13},{10,... | collective-permute-start | bytes 442376 | tf_op jit(solution)/shard_map/ppermute | solution.py:726
  263.6 17.1 %copy-start.9 = (bf16[1,480,768]{2,1,0:T(8,128)(2,1)}, bf16[1,480,768]{2,1,0:T(8,128)(2,1)S(1)}, u32[]{:S(2)}) copy-start(bf16[1,480,768]{2,1,0:T(8,128)(2,1)S(1)} %add_convert_fusion.5.refs_1_) | copy-start | bytes 2211844
  268.3 12.4 %copy-start.27 = (bf16[768,128]{1,0:T(8,128)(2,1)}, bf16[768,128]{1,0:T(8,128)(2,1)S(1)}, u32[]{:S(2)}) copy-start(bf16[768,128]{1,0:T(8,128)(2,1)S(1)} %collective-permute-done.22.refs_9_) | copy-start | bytes 589828
  268.3 36.6 %collective-permute-start.27 = (bf16[2,384,768]{2,1,0:T(8,128)(2,1)S(1)}, bf16[2,384,768]{2,1,0:T(8,128)(2,1)S(1)}, u32[]{:S(2)}, u32[]{:S(2)}) collective-permute-start(bf16[2,384,768]{2,1,0:T(8,128)(2,1)S(1)} %copy-done.31), channel_id=1, source_target_pairs={{0,8},{8,0},{16,24},{24,16},{1,9},{9,1},{17,25},{25,17},{2,10},{10... | collective-permute-start | bytes 3538952 | tf_op jit(solution)/shard_map/ppermute | solution.py:726
  274.4 6.3 %copy-start.28 = (bf16[768,128]{1,0:T(8,128)(2,1)}, bf16[768,128]{1,0:T(8,128)(2,1)S(1)}, u32[]{:S(2)}) copy-start(bf16[768,128]{1,0:T(8,128)(2,1)S(1)} %collective-permute-done.23.refs_10_) | copy-start | bytes 589828
  274.4 17.9 %collective-permute-start.35 = (bf16[1,240,768]{2,1,0:T(8,128)(2,1)S(1)}, bf16[1,240,768]{2,1,0:T(8,128)(2,1)S(1)}, u32[]{:S(2)}, u32[]{:S(2)}) collective-permute-start(bf16[1,240,768]{2,1,0:T(8,128)(2,1)S(1)} %constant_dynamic-slice_fusion.5), channel_id=1, source_target_pairs={{0,2},{1,3},{2,0},{3,1},{4,6},{5,7},{6,4},{7,5},{8,10},{9,11},{10,... | collective-permute-start | bytes 1105928 | tf_op jit(solution)/shard_map/ppermute | solution.py:726
  290.6 29.6 %collective-permute-start.25 = (bf16[2,256,768]{2,1,0:T(8,128)(2,1)}, bf16[2,256,768]{2,1,0:T(8,128)(2,1)S(1)}, u32[]{:S(2)}, u32[]{:S(2)}) collective-permute-start(bf16[2,256,768]{2,1,0:T(8,128)(2,1)} %get-tuple-element.98), channel_id=1, source_target_pairs={{0,8},{8,0},{16,24},{24,16},{1,9},{9,1},{17,25},{25,17},{2,10},{10... | collective-permute-start | bytes 2359304 | tf_op jit(solution)/shard_map/ppermute | solution.py:726
  290.8 9.5 %collective-permute-start.43 = (bf16[1,192,768]{2,1,0:T(8,128)(2,1)S(1)}, bf16[1,192,768]{2,1,0:T(8,128)(2,1)S(1)}, u32[]{:S(2)}, u32[]{:S(2)}) collective-permute-start(bf16[1,192,768]{2,1,0:T(8,128)(2,1)S(1)} %pad_maximum_fusion.8), channel_id=1, source_target_pairs={{0,1},{1,0},{2,3},{3,2},{4,5},{5,4},{6,7},{7,6},{8,9},{9,8},{10,11... | collective-permute-start | bytes 884744 | tf_op jit(solution)/shard_map/ppermute | solution.py:726
  293.4 11.4 %copy-start.16 = (bf16[2,384,768]{2,1,0:T(8,128)(2,1)S(1)}, bf16[2,384,768]{2,1,0:T(8,128)(2,1)}, u32[]{:S(2)}) copy-start(bf16[2,384,768]{2,1,0:T(8,128)(2,1)} %get-tuple-element.99) | copy-start | bytes 3538948
  293.5 11.3 %collective-permute-start.36 = (bf16[1,120,768]{2,1,0:T(8,128)(2,1)S(1)}, bf16[1,120,768]{2,1,0:T(8,128)(2,1)S(1)}, u32[]{:S(2)}, u32[]{:S(2)}) collective-permute-start(bf16[1,120,768]{2,1,0:T(8,128)(2,1)S(1)} %constant_dynamic-slice_fusion.4), channel_id=1, source_target_pairs={{0,4},{1,5},{2,6},{3,7},{4,0},{5,1},{6,2},{7,3},{8,12},{9,13},{10,... | collective-permute-start | bytes 552968 | tf_op jit(solution)/shard_map/ppermute | solution.py:726
  300.4 22.7 %collective-permute-start.44 = (bf16[1,384,768]{2,1,0:T(8,128)(2,1)S(1)}, bf16[1,384,768]{2,1,0:T(8,128)(2,1)S(1)}, u32[]{:S(2)}, u32[]{:S(2)}) collective-permute-start(bf16[1,384,768]{2,1,0:T(8,128)(2,1)S(1)} %pad_maximum_fusion.5), channel_id=1, source_target_pairs={{0,2},{1,3},{2,0},{3,1},{4,6},{5,7},{6,4},{7,5},{8,10},{9,11},{10,... | collective-permute-start | bytes 1769480 | tf_op jit(solution)/shard_map/ppermute | solution.py:726
  304.8 12.3 %collective-permute-start.37 = (bf16[1,120,768]{2,1,0:T(8,128)(2,1)S(1)}, bf16[1,120,768]{2,1,0:T(8,128)(2,1)S(1)}, u32[]{:S(2)}, u32[]{:S(2)}) collective-permute-start(bf16[1,120,768]{2,1,0:T(8,128)(2,1)S(1)} %add_convert_fusion.11), channel_id=1, source_target_pairs={{0,4},{1,5},{2,6},{3,7},{4,0},{5,1},{6,2},{7,3},{8,12},{9,13},{10,... | collective-permute-start | bytes 552968 | tf_op jit(solution)/shard_map/ppermute | solution.py:726
  305.2 15.0 %copy-start.21 = (bf16[2,256,768]{2,1,0:T(8,128)(2,1)S(1)}, bf16[2,256,768]{2,1,0:T(8,128)(2,1)}, u32[]{:S(2)}) copy-start(bf16[2,256,768]{2,1,0:T(8,128)(2,1)} %get-tuple-element.97) | copy-start | bytes 2359300
  305.3 16.0 %collective-permute-start.28 = (bf16[1,384,768]{2,1,0:T(8,128)(2,1)S(1)}, bf16[1,384,768]{2,1,0:T(8,128)(2,1)S(1)}, u32[]{:S(2)}, u32[]{:S(2)}) collective-permute-start(bf16[1,384,768]{2,1,0:T(8,128)(2,1)S(1)} %slice.122), channel_id=1, source_target_pairs={{0,16},{8,24},{16,0},{24,8},{1,17},{9,25},{17,1},{25,9},{2,18},{10... | collective-permute-start | bytes 1769480 | tf_op jit(solution)/shard_map/ppermute | solution.py:726
  317.2 18.9 %collective-permute-start.38 = (bf16[1,240,768]{2,1,0:T(8,128)(2,1)S(1)}, bf16[1,240,768]{2,1,0:T(8,128)(2,1)S(1)}, u32[]{:S(2)}, u32[]{:S(2)}) collective-permute-start(bf16[1,240,768]{2,1,0:T(8,128)(2,1)S(1)} %pad_maximum_fusion.6), channel_id=1, source_target_pairs={{0,2},{1,3},{2,0},{3,1},{4,6},{5,7},{6,4},{7,5},{8,10},{9,11},{10,... | collective-permute-start | bytes 1105928 | tf_op jit(solution)/shard_map/ppermute | solution.py:726
  320.7 27.3 %collective-permute-start.26 = (bf16[256,768]{1,0:T(8,128)(2,1)S(1)}, bf16[256,768]{1,0:T(8,128)(2,1)S(1)}, u32[]{:S(2)}, u32[]{:S(2)}) collective-permute-start(bf16[256,768]{1,0:T(8,128)(2,1)S(1)} %slice_bitcast_fusion), channel_id=1, source_target_pairs={{0,16},{8,24},{16,0},{24,8},{1,17},{9,25},{17,1},{25,9},{2,18},{10... | collective-permute-start | bytes 1179656 | tf_op jit(solution)/shard_map/ppermute | solution.py:726
  321.5 14.0 %collective-permute-start.29 = (bf16[1,192,768]{2,1,0:T(8,128)(2,1)S(1)}, bf16[1,192,768]{2,1,0:T(8,128)(2,1)S(1)}, u32[]{:S(2)}, u32[]{:S(2)}) collective-permute-start(bf16[1,192,768]{2,1,0:T(8,128)(2,1)S(1)} %constant_dynamic-slice_fusion.8), channel_id=1, source_target_pairs={{0,2},{1,3},{2,0},{3,1},{4,6},{5,7},{6,4},{7,5},{8,10},{9,11},{10,... | collective-permute-start | bytes 884744 | tf_op jit(solution)/shard_map/ppermute | solution.py:726
  335.6 5.4 %collective-permute-start.30 = (bf16[1,96,768]{2,1,0:T(8,128)(2,1)S(1)}, bf16[1,96,768]{2,1,0:T(8,128)(2,1)S(1)}, u32[]{:S(2)}, u32[]{:S(2)}) collective-permute-start(bf16[1,96,768]{2,1,0:T(8,128)(2,1)S(1)} %constant_dynamic-slice_fusion.7), channel_id=1, source_target_pairs={{0,1},{1,0},{2,3},{3,2},{4,5},{5,4},{6,7},{7,6},{8,9},{9,8},{10,11... | collective-permute-start | bytes 442376 | tf_op jit(solution)/shard_map/ppermute | solution.py:726
  341.0 6.8 %collective-permute-start.31 = (bf16[1,48,768]{2,1,0:T(8,128)(2,1)S(1)}, bf16[1,48,768]{2,1,0:T(8,128)(2,1)S(1)}, u32[]{:S(2)}, u32[]{:S(2)}) collective-permute-start(bf16[1,48,768]{2,1,0:T(8,128)(2,1)S(1)} %constant_dynamic-slice_fusion.6), channel_id=1, source_target_pairs={{0,4},{1,5},{2,6},{3,7},{4,0},{5,1},{6,2},{7,3},{8,12},{9,13},{10,... | collective-permute-start | bytes 221192 | tf_op jit(solution)/shard_map/ppermute | solution.py:726
  342.9 30.2 %collective-permute-start.39 = (bf16[1,480,768]{2,1,0:T(8,128)(2,1)}, bf16[1,480,768]{2,1,0:T(8,128)(2,1)S(1)}, u32[]{:S(2)}, u32[]{:S(2)}) collective-permute-start(bf16[1,480,768]{2,1,0:T(8,128)(2,1)} %pad_maximum_fusion.4), channel_id=1, source_target_pairs={{0,1},{1,0},{2,3},{3,2},{4,5},{5,4},{6,7},{7,6},{8,9},{9,8},{10,11... | collective-permute-start | bytes 2211848 | tf_op jit(solution)/shard_map/ppermute | solution.py:726
  347.9 6.6 %collective-permute-start.32 = (bf16[1,48,768]{2,1,0:T(8,128)(2,1)S(1)}, bf16[1,48,768]{2,1,0:T(8,128)(2,1)S(1)}, u32[]{:S(2)}, u32[]{:S(2)}) collective-permute-start(bf16[1,48,768]{2,1,0:T(8,128)(2,1)S(1)} %add_convert_fusion.14), channel_id=1, source_target_pairs={{0,4},{1,5},{2,6},{3,7},{4,0},{5,1},{6,2},{7,3},{8,12},{9,13},{10,... | collective-permute-start | bytes 221192 | tf_op jit(solution)/shard_map/ppermute | solution.py:726
  348.8 20.0 %all-to-all-start = ((bf16[8,32,768]{2,1,0:T(8,128)(2,1)}), bf16[8,32,768]{2,1,0:T(8,128)(2,1)S(1)}, u32[]{:S(2)}, u32[]{:S(2)}) async-start(bf16[8,32,768]{2,1,0:T(8,128)(2,1)} %bitcast.15), calls=%async_computation | async-start | bytes 786432 | tf_op jit(solution)/shard_map/all_to_all | solution.py:768
  354.5 12.1 %collective-permute-start.33 = (bf16[1,96,768]{2,1,0:T(8,128)(2,1)S(1)}, bf16[1,96,768]{2,1,0:T(8,128)(2,1)S(1)}, u32[]{:S(2)}, u32[]{:S(2)}) collective-permute-start(bf16[1,96,768]{2,1,0:T(8,128)(2,1)S(1)} %pad_maximum_fusion.9), channel_id=1, source_target_pairs={{0,1},{1,0},{2,3},{3,2},{4,5},{5,4},{6,7},{7,6},{8,9},{9,8},{10,11... | collective-permute-start | bytes 442376 | tf_op jit(solution)/shard_map/ppermute | solution.py:726
  366.7 9.1 %collective-permute-start.34 = (bf16[1,192,768]{2,1,0:T(8,128)(2,1)S(1)}, bf16[1,192,768]{2,1,0:T(8,128)(2,1)S(1)}, u32[]{:S(2)}, u32[]{:S(2)}) collective-permute-start(bf16[1,192,768]{2,1,0:T(8,128)(2,1)S(1)} %pad_maximum_fusion.7), channel_id=1, source_target_pairs={{0,2},{1,3},{2,0},{3,1},{4,6},{5,7},{6,4},{7,5},{8,10},{9,11},{10,... | collective-permute-start | bytes 884744 | tf_op jit(solution)/shard_map/ppermute | solution.py:726
  369.6 13.3 %all-to-all-start.1 = ((bf16[8,32,768]{2,1,0:T(8,128)(2,1)}), bf16[8,32,768]{2,1,0:T(8,128)(2,1)S(1)}, u32[]{:S(2)}, u32[]{:S(2)}) async-start(bf16[8,32,768]{2,1,0:T(8,128)(2,1)} %broadcast_in_dim.15), calls=%async_computation.1 | async-start | bytes 786432 | tf_op jit(solution)/shard_map/all_to_all | solution.py:770
  (16 other events, 36.7 us)
